TPU v7x, 32 devices: a whole 2x2x4 slice. The times are simulated.
32 devices in a mesh: dp: 8 (over z, x), pipe: 2 (over y), tensor: 2 (over core).
Axes of the slice: x: 2, y: 2, z: 4, core: 2. Of those that a mesh axis runs over, the one named last changes fastest.
Arguments:
- ends: bfloat16 [2, 196, 128, 512], P('pipe', 'tensor', 'dp'), may hold values from -6 to 6
- image_counts: int32 [8], P('dp'), may hold values from 8 to 16, as said below
- norm_gains: float32 [2, 2, 512], P('pipe'), may hold values from 0.5 to 1.5
- norm_shifts: float32 [2, 2, 512], P('pipe'), may hold values from -1.5 to 1.5
- w_qkv: bfloat16 [2, 3, 512, 512], P('pipe', None, 'dp', 'tensor'), may hold values from -0.25 to 0.25
- qv_bias: float32 [2, 2, 512], P('pipe', None, 'tensor'), may hold values from -1.5 to 1.5
- rel_table: float32 [2, 16, 169], P('pipe', 'tensor'), may hold values from -4 to 4
- w_proj: bfloat16 [2, 512, 512], P('pipe', 'dp', 'tensor'), may hold values from -0.75 to 0.75
- out_biases: float32 [2, 2, 512], P('pipe'), may hold values from -1.5 to 1.5
- w_fc1: bfloat16 [2, 512, 2048], P('pipe', 'dp', 'tensor'), may hold values from -0.25 to 0.25
- fc1_bias: float32 [2, 2048], P('pipe', 'tensor'), may hold values from -1.5 to 1.5
- w_fc2: bfloat16 [2, 512, 2048], P('pipe', 'dp', 'tensor'), may hold values from -0.125 to 0.125
Outputs:
- section_input_grads: bfloat16 [2, 196, 128, 512], P('pipe', 'tensor', 'dp')
- norm_gains_grad: float32 [2, 2, 512], P('pipe')
- norm_shifts_grad: float32 [2, 2, 512], P('pipe')
- w_qkv_grad: float32 [2, 3, 512, 512], P('pipe', None, 'dp', 'tensor')
- qv_bias_grad: float32 [2, 2, 512], P('pipe', None, 'tensor')
- rel_table_grad: float32 [2, 16, 169], P('pipe', 'tensor')
- w_proj_grad: float32 [2, 512, 512], P('pipe', 'dp', 'tensor')
- out_biases_grad: float32 [2, 2, 512], P('pipe')
- w_fc1_grad: float32 [2, 512, 2048], P('pipe', 'dp', 'tensor')
- fc1_bias_grad: float32 [2, 2048], P('pipe', 'tensor')
- w_fc2_grad: float32 [2, 512, 2048], P('pipe', 'dp', 'tensor')
Inputs may be any that keep to these rules, and one draw needn't show every extreme that they name: Data shard d holds 16 image slots, of which the first image_counts[d] are real; some shard is full.
All inputs are finite; a program needn't handle non-finite values.
Results may differ from a plain program's by a relative error of at most 0.029.
Values may be sent and summed in bfloat16 or wider, within the bound.
A program may use at most 256 MiB of HBM per device.

v0:
```python
from functools import partial

import jax
import jax.numpy as jnp
from jax import lax
from jax.sharding import PartitionSpec as P

D = 512
SIDE = 14
WIN = 7
SHIFT = 3
MICRO = 2


HIGHEST = lax.Precision.HIGHEST


def passed_along(array, axis, by):
    size = lax.axis_size(axis)
    pairs = [(i, i + by) for i in range(size) if 0 <= i + by < size]
    return lax.ppermute(array, axis, pairs)


def window_tables():
    places = jnp.arange(WIN * WIN, dtype=jnp.int32)
    rows_in = places // WIN
    cols_in = places % WIN
    rel_index = (rows_in[:, None] - rows_in[None, :] + WIN - 1) * (2 * WIN - 1) + (
        cols_in[:, None] - cols_in[None, :] + WIN - 1
    )
    per_side = SIDE // WIN
    windows = jnp.arange(per_side * per_side, dtype=jnp.int32)
    grid_row = (windows // per_side)[:, None] * WIN + rows_in[None, :]
    grid_col = (windows % per_side)[:, None] * WIN + cols_in[None, :]

    def region(position):
        return (position >= SIDE - WIN).astype(jnp.int32) + (position >= SIDE - SHIFT).astype(
            jnp.int32
        )

    labels = 3 * region(grid_row) + region(grid_col)
    region_mask = jnp.where(labels[:, :, None] != labels[:, None, :], -100.0, 0.0).astype(
        jnp.float32
    )
    return (rel_index, region_mask)


def layer_norm(values, gain_row, shift_row):
    center = values - jnp.mean(values, axis=-1, keepdims=True)
    spread = jnp.mean(center * center, axis=-1, keepdims=True)
    return center * lax.rsqrt(spread + 1e-05) * gain_row + shift_row


def roll_grid(grid_in, first_place):
    doubled = jnp.concatenate([grid_in, grid_in], axis=0)
    grid_in = lax.dynamic_slice_in_dim(doubled, first_place, SIDE, 0)
    doubled = jnp.concatenate([grid_in, grid_in], axis=1)
    return lax.dynamic_slice_in_dim(doubled, first_place, SIDE, 1)


def to_windows(tokens_seq, offset):
    images_mb = tokens_seq.shape[1]
    feature_n = tokens_seq.shape[2]
    per_side = SIDE // WIN
    grid_view = roll_grid(tokens_seq.reshape(SIDE, SIDE, images_mb, feature_n), offset)
    grid_view = grid_view.reshape(per_side, WIN, per_side, WIN, images_mb, feature_n).transpose(
        4, 0, 2, 1, 3, 5
    )
    return grid_view.reshape(images_mb * per_side * per_side, WIN * WIN, feature_n)


def from_windows(blocks, offset, images_mb):
    feature_n = blocks.shape[-1]
    per_side = SIDE // WIN
    grid_view = blocks.reshape(images_mb, per_side, per_side, WIN, WIN, feature_n).transpose(
        1, 3, 2, 4, 0, 5
    )
    grid_view = roll_grid(grid_view.reshape(SIDE, SIDE, images_mb, feature_n), SIDE - offset)
    return grid_view.reshape(SIDE * SIDE, images_mb, feature_n)


def on_device(
    ends,
    image_counts,
    norm_gains,
    norm_shifts,
    w_qkv,
    qv_bias,
    rel_table,
    w_proj,
    out_biases,
    w_fc1,
    fc1_bias,
    w_fc2,
):
    section_index = lax.axis_index("pipe")
    is_first = section_index == 0
    offset = SHIFT * section_index
    mask_weight = section_index.astype(jnp.float32)
    rel_index, region_mask = window_tables()
    one_hot = (
        rel_index.reshape(-1)[:, None]
        == jnp.arange((2 * WIN - 1) * (2 * WIN - 1), dtype=jnp.int32)[None, :]
    ).astype(jnp.float32)
    qkv_full, proj_full, fc1_full, fc2_full = (
        lax.all_gather(w_qkv, "dp", axis=2, tiled=True),
        lax.all_gather(w_proj, "dp", axis=1, tiled=True),
        lax.all_gather(w_fc1, "dp", axis=1, tiled=True),
        lax.all_gather(w_fc2, "dp", axis=1, tiled=True),
    )
    bias_pair, table_part, hidden_part = (qv_bias, rel_table, fc1_bias)
    slot_base = 0
    qkv_weight = qkv_full[0]
    proj_weight = proj_full[0]
    fc1_weight = fc1_full[0]
    fc2_weight = fc2_full[0]
    gain_one = norm_gains[0, 0]
    gain_two = norm_gains[0, 1]
    shift_one = norm_shifts[0, 0]
    shift_two = norm_shifts[0, 1]
    q_bias = bias_pair[0, 0]
    v_bias = bias_pair[0, 1]
    bias_table = table_part[0]
    proj_bias = out_biases[0, 0]
    fc2_bias = out_biases[0, 1]
    hidden_bias = hidden_part[0]
    heads_here = bias_table.shape[0]
    qkv_width = qkv_weight.shape[2]
    head_size = qkv_width // heads_here
    q_scale = head_size ** (-0.5)
    rel_bias = jnp.dot(bias_table, one_hot.T, precision=HIGHEST).reshape(
        heads_here, WIN * WIN, WIN * WIN
    )
    own_rows = ends[0]
    row_count = own_rows.shape[0]
    capacity = own_rows.shape[1]
    images_mb = capacity // MICRO
    real_mask = (slot_base + jnp.arange(capacity, dtype=jnp.int32) < image_counts[0]).astype(
        jnp.float32
    )
    win_mask = jnp.tile(region_mask, (images_mb, 1, 1))[:, None] * mask_weight

    def split_heads(blocks):
        return blocks.reshape(blocks.shape[0], blocks.shape[1], heads_here, head_size)

    def split_qkv(windowed):
        query_w = split_heads(windowed[:, :, :qkv_width])
        key_w = split_heads(windowed[:, :, qkv_width : 2 * qkv_width])
        value_w = split_heads(windowed[:, :, 2 * qkv_width :])
        return (query_w, key_w, value_w)

    def scores_of(query_w, key_w):
        raw_scores = jnp.einsum(
            "wqhe,wkhe->whqk", query_w, key_w, preferred_element_type=jnp.float32
        )
        return raw_scores + rel_bias[None] + win_mask

    micro_inputs = [
        own_rows[:, number * images_mb : (number + 1) * images_mb] for number in range(MICRO)
    ]
    micro_cots = [
        micro_inputs[number].astype(jnp.float32)
        * real_mask[number * images_mb : (number + 1) * images_mb][None, :, None]
        for number in range(MICRO)
    ]
    incoming = jnp.zeros_like(micro_inputs[0])
    saved_ticks = []
    for tick_no in range(MICRO + 1):
        section_feed = jnp.where(is_first, micro_inputs[min(tick_no, MICRO - 1)], incoming)
        forward_values = section_feed.astype(jnp.float32)
        normed = layer_norm(forward_values, gain_one, shift_one).astype(jnp.bfloat16)
        forward_normed_full = lax.all_gather(normed, "tensor", axis=0, tiled=True)
        projected = jnp.einsum(
            "sbd,cde->sbce", forward_normed_full, qkv_weight, preferred_element_type=jnp.float32
        )
        queries = ((projected[:, :, 0] + q_bias) * q_scale).astype(jnp.bfloat16)
        keys_seq = projected[:, :, 1].astype(jnp.bfloat16)
        values_seq = (projected[:, :, 2] + v_bias).astype(jnp.bfloat16)
        forward_windowed = to_windows(
            jnp.concatenate([queries, keys_seq, values_seq], axis=2), offset
        )
        forward_query_w, forward_key_w, forward_value_w = split_qkv(forward_windowed)
        scores = scores_of(forward_query_w, forward_key_w)
        row_max = jnp.max(scores, axis=-1, keepdims=True)
        forward_log_total = row_max + jnp.log(
            jnp.sum(jnp.exp(scores - row_max), axis=-1, keepdims=True)
        )
        forward_attn_probs = jnp.exp(scores - forward_log_total).astype(jnp.bfloat16)
        attended = jnp.einsum(
            "whqk,wkhe->wqhe",
            forward_attn_probs,
            forward_value_w,
            preferred_element_type=jnp.float32,
        ).astype(jnp.bfloat16)
        forward_attended_seq = from_windows(
            attended.reshape(attended.shape[0], WIN * WIN, qkv_width), offset, images_mb
        )
        branch = (
            lax.psum_scatter(
                jnp.einsum(
                    "sbe,de->sbd",
                    forward_attended_seq,
                    proj_weight,
                    preferred_element_type=jnp.float32,
                ).astype(jnp.bfloat16),
                "tensor",
                scatter_dimension=0,
                tiled=True,
            ).astype(jnp.float32)
            + proj_bias
        )
        forward_middle = forward_values + branch
        normed_two = layer_norm(forward_middle, gain_two, shift_two).astype(jnp.bfloat16)
        forward_normed_two_full = lax.all_gather(normed_two, "tensor", axis=0, tiled=True)
        forward_hidden_pre = (
            jnp.einsum(
                "sbd,df->sbf",
                forward_normed_two_full,
                fc1_weight,
                preferred_element_type=jnp.float32,
            )
            + hidden_bias
        )
        forward_hidden = jax.nn.gelu(forward_hidden_pre, approximate=False).astype(jnp.bfloat16)
        mlp_sum = lax.psum_scatter(
            jnp.einsum(
                "sbf,df->sbd", forward_hidden, fc2_weight, preferred_element_type=jnp.float32
            ).astype(jnp.bfloat16),
            "tensor",
            scatter_dimension=0,
            tiled=True,
        ).astype(jnp.float32)
        result = forward_middle + (mlp_sum + fc2_bias)
        forward_kept_state = (
            forward_values,
            forward_normed_full,
            forward_windowed,
            forward_log_total,
            forward_attended_seq,
            forward_middle,
            forward_normed_two_full,
            forward_hidden_pre,
        )
        result, kept_state = (result.astype(jnp.bfloat16), forward_kept_state)
        saved_ticks.append(kept_state)
        if tick_no < MICRO:
            incoming = passed_along(result, "pipe", 1)
    kept_list = [
        jax.tree.map(
            lambda early_one, late_one: jnp.where(is_first, early_one, late_one),
            saved_ticks[number],
            saved_ticks[number + 1],
        )
        for number in range(MICRO)
    ]
    incoming_grad = jnp.zeros((row_count, images_mb, D), jnp.float32)
    grad_ticks = []
    for tick_no in range(MICRO + 1):
        late_no = min(tick_no, MICRO - 1)
        early_no = max(tick_no - 1, 0)
        restored = jax.tree.map(
            lambda early_one, late_one: jnp.where(is_first, early_one, late_one),
            kept_list[early_no],
            kept_list[late_no],
        )
        grad_in = jnp.where(is_first, incoming_grad, micro_cots[late_no])
        (
            values,
            normed_full,
            backward_windowed,
            log_total,
            attended_seq,
            middle,
            normed_two_full,
            hidden_pre,
        ) = restored
        grad_branch = grad_in.astype(jnp.bfloat16)
        fc2_bias_grad = jnp.sum(grad_branch.astype(jnp.float32), axis=(0, 1))
        grad_branch_full = lax.all_gather(grad_branch, "tensor", axis=0, tiled=True)
        hidden, gelu_back = jax.vjp(partial(jax.nn.gelu, approximate=False), hidden_pre)
        hidden = hidden.astype(jnp.bfloat16)
        fc2_grad = jnp.einsum(
            "sbd,sbf->df", grad_branch_full, hidden, preferred_element_type=jnp.float32
        )
        grad_hidden = jnp.einsum(
            "sbd,df->sbf", grad_branch_full, fc2_weight, preferred_element_type=jnp.float32
        )
        grad_pre = gelu_back(grad_hidden)[0].astype(jnp.bfloat16)
        hidden_bias_grad = jnp.sum(grad_pre.astype(jnp.float32), axis=(0, 1))
        fc1_grad = jnp.einsum(
            "sbd,sbf->df", normed_two_full, grad_pre, preferred_element_type=jnp.float32
        )
        grad_normed_two = lax.psum_scatter(
            jnp.einsum(
                "sbf,df->sbd", grad_pre, fc1_weight, preferred_element_type=jnp.float32
            ).astype(jnp.bfloat16),
            "tensor",
            scatter_dimension=0,
            tiled=True,
        ).astype(jnp.float32)
        norm_two_out, norm_two_back = jax.vjp(layer_norm, middle, gain_two, shift_two)
        grad_middle_part, gain_two_grad, shift_two_grad = norm_two_back(grad_normed_two)
        grad_middle = grad_in + grad_middle_part
        grad_attn = grad_middle.astype(jnp.bfloat16)
        proj_bias_grad = jnp.sum(grad_attn.astype(jnp.float32), axis=(0, 1))
        grad_attn_full = lax.all_gather(grad_attn, "tensor", axis=0, tiled=True)
        proj_grad = jnp.einsum(
            "sbd,sbe->de", grad_attn_full, attended_seq, preferred_element_type=jnp.float32
        )
        grad_attended = jnp.einsum(
            "sbd,de->sbe", grad_attn_full, proj_weight, preferred_element_type=jnp.float32
        ).astype(jnp.bfloat16)
        grad_att_w = split_heads(to_windows(grad_attended, offset))
        backward_query_w, backward_key_w, backward_value_w = split_qkv(backward_windowed)
        attn_probs = jnp.exp(scores_of(backward_query_w, backward_key_w) - log_total)
        grad_probs = jnp.einsum(
            "wqhe,wkhe->whqk", grad_att_w, backward_value_w, preferred_element_type=jnp.float32
        )
        grad_scores = (
            attn_probs * (grad_probs - jnp.sum(attn_probs * grad_probs, axis=-1, keepdims=True))
        ).astype(jnp.bfloat16)
        score_sum = jnp.sum(grad_scores.astype(jnp.float32), axis=0).reshape(
            heads_here, WIN * WIN * WIN * WIN
        )
        table_grad = jnp.dot(score_sum, one_hot, precision=HIGHEST)
        grad_query = (
            jnp.einsum(
                "whqk,wkhe->wqhe", grad_scores, backward_key_w, preferred_element_type=jnp.float32
            )
            * q_scale
        ).astype(jnp.bfloat16)
        grad_key = jnp.einsum(
            "whqk,wqhe->wkhe", grad_scores, backward_query_w, preferred_element_type=jnp.float32
        ).astype(jnp.bfloat16)
        grad_value = jnp.einsum(
            "whqk,wqhe->wkhe",
            attn_probs.astype(jnp.bfloat16),
            grad_att_w,
            preferred_element_type=jnp.float32,
        ).astype(jnp.bfloat16)
        windows_n = backward_windowed.shape[0]
        grad_stack = jnp.concatenate(
            [
                grad_query.reshape(windows_n, WIN * WIN, qkv_width),
                grad_key.reshape(windows_n, WIN * WIN, qkv_width),
                grad_value.reshape(windows_n, WIN * WIN, qkv_width),
            ],
            axis=2,
        )
        grad_seq = from_windows(grad_stack, offset, images_mb).reshape(
            SIDE * SIDE, images_mb, 3, qkv_width
        )
        q_bias_grad = jnp.sum(grad_seq[:, :, 0].astype(jnp.float32), axis=(0, 1))
        v_bias_grad = jnp.sum(grad_seq[:, :, 2].astype(jnp.float32), axis=(0, 1))
        qkv_grad = jnp.einsum(
            "sbd,sbce->cde", normed_full, grad_seq, preferred_element_type=jnp.float32
        )
        grad_normed = lax.psum_scatter(
            jnp.einsum(
                "sbce,cde->sbd", grad_seq, qkv_weight, preferred_element_type=jnp.float32
            ).astype(jnp.bfloat16),
            "tensor",
            scatter_dimension=0,
            tiled=True,
        ).astype(jnp.float32)
        norm_one_out, norm_one_back = jax.vjp(layer_norm, values, gain_one, shift_one)
        grad_values_part, gain_one_grad, shift_one_grad = norm_one_back(grad_normed)
        grad_values = grad_middle + grad_values_part
        matrix_grads = (qkv_grad, proj_grad, fc1_grad, fc2_grad)
        shared_part = (
            jnp.stack([gain_one_grad, gain_two_grad]),
            jnp.stack([shift_one_grad, shift_two_grad]),
            jnp.stack([proj_bias_grad, fc2_bias_grad]),
        )
        head_part = (jnp.stack([q_bias_grad, v_bias_grad]), hidden_bias_grad, table_grad)
        grad_values, matrix_grads, shared_part, head_part = (
            grad_values,
            matrix_grads,
            shared_part,
            head_part,
        )
        weight_now = jnp.where(
            is_first, 1.0 if tick_no >= 1 else 0.0, 1.0 if tick_no < MICRO else 0.0
        ).astype(jnp.float32)
        matrix_grads = jax.tree.map(lambda grad_term: grad_term * weight_now, matrix_grads)
        shared_part = jax.tree.map(lambda grad_term: grad_term * weight_now, shared_part)
        head_part = jax.tree.map(lambda grad_term: grad_term * weight_now, head_part)
        if tick_no == 0:
            matrix_total, shared_total, head_total = (matrix_grads, shared_part, head_part)
        else:
            matrix_total = jax.tree.map(jnp.add, matrix_total, matrix_grads)
            shared_total = jax.tree.map(jnp.add, shared_total, shared_part)
            head_total = jax.tree.map(jnp.add, head_total, head_part)
        grad_ticks.append(grad_values)
        if tick_no < MICRO:
            incoming_grad = passed_along(grad_values.astype(jnp.bfloat16), "pipe", -1).astype(
                jnp.float32
            )
    matrix_parts = matrix_total
    matrix_parts = (
        lax.psum_scatter(matrix_parts[0], "dp", scatter_dimension=1, tiled=True),
        lax.psum_scatter(matrix_parts[1], "dp", scatter_dimension=0, tiled=True),
        lax.psum_scatter(matrix_parts[2], "dp", scatter_dimension=0, tiled=True),
        lax.psum_scatter(matrix_parts[3], "dp", scatter_dimension=0, tiled=True),
    )
    matrix_total, head_total = (matrix_parts, head_total)
    shared_sum = lax.psum((shared_total[0], shared_total[1], shared_total[2]), ("dp", "tensor"))
    head_sum = lax.psum((head_total[0], head_total[1], head_total[2]), "dp")
    section_parts = [
        jnp.where(is_first, grad_ticks[number + 1], grad_ticks[number]) for number in range(MICRO)
    ]
    section_grads = jnp.concatenate(section_parts, axis=1).astype(jnp.bfloat16)[None]
    return (
        section_grads,
        shared_sum[0][None],
        shared_sum[1][None],
        matrix_total[0][None],
        head_sum[0][None],
        head_sum[2][None],
        matrix_total[1][None],
        shared_sum[2][None],
        matrix_total[2][None],
        head_sum[1][None],
        matrix_total[3][None],
    )


def solution(mesh):
    return jax.shard_map(
        on_device,
        mesh=mesh,
        in_specs=(
            P("pipe", "tensor", "dp", None),
            P("dp"),
            P("pipe", None, None),
            P("pipe", None, None),
            P("pipe", None, "dp", "tensor"),
            P("pipe", None, "tensor"),
            P("pipe", "tensor", None),
            P("pipe", "dp", "tensor"),
            P("pipe", None, None),
            P("pipe", "dp", "tensor"),
            P("pipe", "tensor"),
            P("pipe", "dp", "tensor"),
        ),
        out_specs=(
            P("pipe", "tensor", "dp", None),
            P("pipe", None, None),
            P("pipe", None, None),
            P("pipe", None, "dp", "tensor"),
            P("pipe", None, "tensor"),
            P("pipe", "tensor", None),
            P("pipe", "dp", "tensor"),
            P("pipe", None, None),
            P("pipe", "dp", "tensor"),
            P("pipe", "tensor"),
            P("pipe", "dp", "tensor"),
        ),
        check_vma=False,
    )
```

profile of v0, /device:TPU:0, one launch (start us, length us, event | category | flops | bytes accessed | tf_op | source)
XLA Modules:
  0.0 1325.6 jit_solution(8660555740009630731)
XLA Ops:
  16.5 32.6 %all_gather.50 = bf16[1,512,256]{2,1,0:T(8,128)(2,1)S(1)} all-gather(bf16[1,64,256]{2,1,0:T(8,128)(2,1)S(1)} %copy-done.117), channel_id=1, replica_groups=mesh['dp'=8,'pipe'=2,'tensor'=2] {'dp'}, dimensions={1}, use_global_device_ids=true | all-gather | bytes 294912 | tf_op jit(solution)/shard_map/all_gather | solution.py:107
  49.3 31.7 %all_gather.49 = bf16[1,3,512,256]{3,2,1,0:T(8,128)(2,1)S(1)} all-gather(bf16[1,3,64,256]{3,2,1,0:T(8,128)(2,1)S(1)} %copy-done.115), channel_id=1, replica_groups=mesh['dp'=8,'pipe'=2,'tensor'=2] {'dp'}, dimensions={2}, use_global_device_ids=true | all-gather | bytes 884736 | tf_op jit(solution)/shard_map/all_gather | solution.py:106
  124.9 7.3 copy.215
  143.0 10.1 reduce-scatter.15.cloned.1.call-done
  158.6 28.3 %all-gather.19.cloned.1.call-done = bf16[1,512,1024]{2,1,0:T(8,128)(2,1)} async-done(((bf16[1,64,1024]{2,1,0:T(8,128)(2,1)}), bf16[1,512,1024]{2,1,0:T(8,128)(2,1)}) %all-gather.19.cloned.1.call-update) | async-done | bytes 1048592 | tf_op jit(solution)/shard_map/all_gather | solution.py:108
  186.9 10.3 all-gather.17.cloned.1.call-done
  203.5 37.4 %all-gather.21.cloned.1.call-done = bf16[1,512,1024]{2,1,0:T(8,128)(2,1)} async-done(((bf16[1,64,1024]{2,1,0:T(8,128)(2,1)}), bf16[1,512,1024]{2,1,0:T(8,128)(2,1)}) %all-gather.21.cloned.1.call-update) | async-done | bytes 1048592 | tf_op jit(solution)/shard_map/all_gather | solution.py:109
  240.8 17.3 %fusion.134 = bf16[196,8,512]{2,1,0:T(8,128)(2,1)} fusion(f32[196,8,1024]{2,1,0:T(8,128)} %fusion.221, f32[1024]{0:T(1024)S(1)} %bitcast.633, bf16[1,512,1024]{2,1,0:T(8,128)(2,1)} %all-gather.21.cloned.1.call-done), kind=kOutput, calls=%fused_computation.301 | convolution fusion | flops 1750941696 | bytes 9080832 | tf_op jit(solution)/shard_map/sbf,df->sbd/dot_general | solution.py:226
  258.2 7.7 reduce-scatter.17.cloned.1.call-done
  271.3 17.5 %collective-permute-done = bf16[98,8,512]{2,1,0:T(8,128)(2,1)S(1)} collective-permute-done((bf16[98,8,512]{2,1,0:T(8,128)(2,1)S(1)}, bf16[98,8,512]{2,1,0:T(8,128)(2,1)S(1)}, u32[]{:S(2)}, u32[]{:S(2)}) %collective-permute-start) | collective-permute-done | bytes 802848 | tf_op jit(solution)/shard_map/ppermute | solution.py:21
  290.9 11.7 all-gather.23.cloned.1.call-done
  347.8 7.2 copy.222
  366.6 9.1 reduce-scatter.19.cloned.1.call-done
  384.1 10.6 all-gather.25.cloned.1.call-done
  394.7 18.6 %fusion.3 = (f32[196,8,1024]{2,1,0:T(8,128)}, f32[196,8,1024]{2,1,0:T(8,128)}, f32[196,8,1024]{2,1,0:T(8,128)S(1)}) fusion(f32[196,8,1024]{2,1,0:T(8,128)} %fusion.221, f32[1024]{0:T(1024)S(1)} %bitcast.634, pred[]{:T(512)S(6)} %eq.38, bf16[196,8,512]{2,1,0:T(8,128)(2,1)} %all-gather.25.cloned.1.call-done, ...), kind=kOutput, calls=%fused_computation.29 | convolution fusion | flops 1748533248 | bytes 28348416 | tf_op jit(solution)/shard_map/sbd,df->sbf/dot_general | solution.py:216
  415.9 15.2 %fusion.137 = bf16[196,8,512]{2,1,0:T(8,128)(2,1)} fusion(f32[196,8,1024]{2,1,0:T(8,128)S(1)} %get-tuple-element.208, f32[1024]{0:T(1024)S(1)} %bitcast.635, bf16[1,512,1024]{2,1,0:T(8,128)(2,1)S(1)} %copy-done.149), kind=kOutput, calls=%fused_computation.302 | convolution fusion | flops 1750941696 | bytes 9080832 | tf_op jit(solution)/shard_map/sbf,df->sbd/dot_general | solution.py:226
  431.4 9.9 convert_reduce_fusion.5
  461.0 10.3 collective-permute-done.2
  477.4 12.1 all-gather.31.cloned.1.call-done
  557.4 11.8 multiply_reduce_fusion.2
  569.2 10.8 convert_reduce_fusion.2
  590.9 7.2 copy.242
  613.6 7.4 copy.230
  632.6 7.3 copy.232
  652.5 7.2 copy.235
  677.9 8.8 reduce-scatter.23.cloned.1.call-done
  703.7 19.6 %collective-permute-done.1 = bf16[98,8,512]{2,1,0:T(8,128)(2,1)S(1)} collective-permute-done((bf16[98,8,512]{2,1,0:T(8,128)(2,1)}, bf16[98,8,512]{2,1,0:T(8,128)(2,1)S(1)}, u32[]{:S(2)}, u32[]{:S(2)}) %collective-permute-start.1) | collective-permute-done | bytes 802848 | tf_op jit(solution)/shard_map/ppermute | solution.py:21
  725.3 32.6 %fusion.7 = (f32[196,8,1024]{2,1,0:T(8,128)}, f32[196,8,1024]{2,1,0:T(8,128)}, f32[196,8,1024]{2,1,0:T(8,128)}, f32[196,8,1024]{2,1,0:T(8,128)}) fusion(f32[196,8,1024]{2,1,0:T(8,128)} %get-tuple-element.143, pred[]{:T(512)S(6)} %eq.38, bf16[196,8,512]{2,1,0:T(8,128)(2,1)} %all-gather.33.cloned.1.call-done, bf16[1,512,1024]{2,1,0:T(8,128)(2,1)S(1)} %copy-done.147, ...), kind=kOutput, calls=%fused_computation.33 | convolution fusion | flops 1849688064 | bytes 41193472 | tf_op jit(solution)/shard_map/sbd,df->sbf/dot_general | solution.py:216
  758.0 8.0 convert_reduce_fusion.4
  771.1 8.8 fusion.71
  803.1 7.4 fusion.379
  822.9 7.7 multiply_reduce_fusion.1
  844.1 7.2 copy.250
  856.2 7.3 copy.252
  868.2 7.3 copy.255
  922.7 7.3 fusion.380
  936.1 8.4 all-gather.39.cloned.1.call-done
  944.5 9.9 convert_reduce_fusion.3
  959.3 8.7 fusion.72
  999.5 7.5 multiply_reduce_fusion
  1020.4 7.3 copy.263
  1032.9 7.3 copy.265
  1045.0 7.2 copy.268
  1077.5 9.5 fusion.108
  1107.1 38.7 %all-reduce.2 = (f32[1,2,256]{2,1,0:T(2,128)}, f32[1,8,169]{2,1,0:T(8,128)}, f32[1,1024]{1,0:T(1,128)}) all-reduce(f32[1,2,256]{2,1,0:T(2,128)S(1)} %fusion.281, f32[1,8,169]{2,1,0:T(8,128)S(1)} %fusion.208, f32[1,1024]{1,0:T(1,128)S(1)} %bitcast.605), channel_id=1, replica_groups=mesh['dp'=8,'pipe'=2,'tensor'=2] {'dp'}, use_global_device_ids=true, to_apply=%region_77.78 | all-reduce | flops 2888 | bytes 23104 | tf_op jit(solution)/shard_map/psum | solution.py:408
  1145.7 37.4 %all-reduce.5.cloned.1.call-done = f32[3,512,256]{2,0,1:T(4,128)} async-done(((f32[3,512,256]{2,0,1:T(4,128)}), f32[3,512,256]{2,0,1:T(4,128)}) %all-reduce.5.cloned.1.call-update) | async-done | bytes 1572880
  1189.6 59.9 %all-reduce.1 = (f32[1,2,512]{2,1,0:T(2,128)}, f32[1,2,512]{2,1,0:T(2,128)}, f32[1,2,512]{2,1,0:T(2,128)}) all-reduce(f32[1,2,512]{2,1,0:T(2,128)S(1)} %fusion.272, f32[1,2,512]{2,1,0:T(2,128)S(1)} %fusion.275, f32[1,2,512]{2,1,0:T(2,128)S(1)} %fusion.278), channel_id=1, replica_groups=mesh['dp'=8,'pipe'=2,'tensor'=2] {'dp','tensor'}, use_global_device_ids=true, to_apply=%region_62.63 | all-reduce | flops 3072 | bytes 24576 | tf_op jit(solution)/shard_map/psum | solution.py:407
  1255.1 62.9 %reduce-scatter.37.cloned.1.call-done = f32[64,256]{1,0:T(8,128)} async-done(((f32[512,256]{1,0:T(8,128)}), f32[64,256]{1,0:T(8,128)}) %reduce-scatter.37.cloned.1.call-update) | async-done | bytes 65552 | tf_op jit(solution)/shard_map/reduce_scatter | solution.py:402
  (659 shorter events, 562.6 us)
Async XLA Ops:
  8.0 73.0 %all-gather.15.cloned.1.call-start = ((), (), s32[]{:S(2)}) async-start(), calls=%async_computation.14 | async-start | bytes 2408448 | tf_op jit(solution)/shard_map/all_gather | solution.py:172
  12.0 685.3 %copy-start.97 = (f32[1,1,512]{2,1,0:T(1,128)}, f32[1,1,512]{2,1,0:T(1,128)S(1)}, u32[]{:S(2)}) copy-start(f32[1,1,512]{2,1,0:T(1,128)S(1)} %get-tuple-element.196) | copy-start | bytes 6148
  12.0 685.3 %copy-start.108 = (f32[1,1,512]{2,1,0:T(1,128)}, f32[1,1,512]{2,1,0:T(1,128)S(1)}, u32[]{:S(2)}) copy-start(f32[1,1,512]{2,1,0:T(1,128)S(1)} %get-tuple-element.197) | copy-start | bytes 6148
  12.7 369.3 %copy-start.118 = (f32[1,1,512]{2,1,0:T(1,128)}, f32[1,1,512]{2,1,0:T(1,128)S(1)}, u32[]{:S(2)}) copy-start(f32[1,1,512]{2,1,0:T(1,128)S(1)} %get-tuple-element.198) | copy-start | bytes 6148
  14.0 139.1 %reduce-scatter.15.cloned.1.call-start = ((), (), s32[]{:S(2)}) async-start(), calls=%async_computation.15 | async-start | bytes 2408448 | tf_op jit(solution)/shard_map/reduce_scatter | solution.py:199
  16.5 101.3 %copy-start.14 = (f32[8,49,49]{1,2,0:T(8,128)}, f32[8,49,49]{1,2,0:T(8,128)S(1)}, u32[]{:S(2)}) copy-start(f32[8,49,49]{1,2,0:T(8,128)S(1)} %copy.213) | copy-start | bytes 230500
  49.1 90.6 %copy-start.42 = (bf16[1,512,256]{2,1,0:T(8,128)(2,1)}, bf16[1,512,256]{2,1,0:T(8,128)(2,1)S(1)}, u32[]{:S(2)}) copy-start(bf16[1,512,256]{2,1,0:T(8,128)(2,1)S(1)} %all_gather.50) | copy-start | bytes 786436
  106.8 538.7 %copy-start.2 = (f32[8,4,49,49]{2,3,1,0:T(8,128)}, f32[8,4,49,49]{2,3,1,0:T(8,128)S(1)}, u32[]{:S(2)}) copy-start(f32[8,4,49,49]{2,3,1,0:T(8,128)S(1)} %tile.2) | copy-start | bytes 921988
  142.4 44.6 %all-gather.19.cloned.1.call-start = ((), (), s32[]{:S(2)}) async-start(), calls=%async_computation.17 | async-start | bytes 1179648 | tf_op jit(solution)/shard_map/all_gather | solution.py:108
  142.9 54.3 %all-gather.17.cloned.1.call-start = ((), (), s32[]{:S(2)}) async-start(), calls=%async_computation.16 | async-start | bytes 2408448 | tf_op jit(solution)/shard_map/all_gather | solution.py:214
  158.0 82.9 %all-gather.21.cloned.1.call-start = ((), (), s32[]{:S(2)}) async-start(), calls=%async_computation.18 | async-start | bytes 1179648 | tf_op jit(solution)/shard_map/all_gather | solution.py:109
  158.5 82.3 %copy-start.151 = (f32[1,1024]{1,0:T(1,128)S(1)}, f32[1,1024]{1,0:T(1,128)}, u32[]{:S(2)}) copy-start(f32[1,1024]{1,0:T(1,128)} %param.22) | copy-start | bytes 12292
  158.6 107.4 %reduce-scatter.17.cloned.1.call-start = ((), (), s32[]{:S(2)}) async-start(), calls=%async_computation.19 | async-start | bytes 2408448 | tf_op jit(solution)/shard_map/reduce_scatter | solution.py:225
  258.2 44.5 %all-gather.23.cloned.1.call-start = ((), (), s32[]{:S(2)}) async-start(), calls=%async_computation.20 | async-start | bytes 2408448 | tf_op jit(solution)/shard_map/all_gather | solution.py:172
  267.5 21.3 %collective-permute-start = (bf16[98,8,512]{2,1,0:T(8,128)(2,1)S(1)}, bf16[98,8,512]{2,1,0:T(8,128)(2,1)S(1)}, u32[]{:S(2)}, u32[]{:S(2)}) collective-permute-start(bf16[98,8,512]{2,1,0:T(8,128)(2,1)S(1)} %add_convert_fusion.8), channel_id=1, source_target_pairs={{0,2},{1,3},{4,6},{5,7},{8,10},{9,11},{12,14},{13,15},{16,18},{17,... | collective-permute-start | bytes 2408456 | tf_op jit(solution)/shard_map/ppermute | solution.py:21
  289.1 408.1 %copy-start.8 = (bf16[98,8,512]{2,1,0:T(8,128)(2,1)}, bf16[98,8,512]{2,1,0:T(8,128)(2,1)S(1)}, u32[]{:S(2)}) copy-start(bf16[98,8,512]{2,1,0:T(8,128)(2,1)S(1)} %get-tuple-element.145) | copy-start | bytes 2408452
  290.9 84.8 %reduce-scatter.19.cloned.1.call-start = ((), (), s32[]{:S(2)}) async-start(), calls=%async_computation.21 | async-start | bytes 2408448 | tf_op jit(solution)/shard_map/reduce_scatter | solution.py:199
  365.3 29.3 %all-gather.25.cloned.1.call-start = ((), (), s32[]{:S(2)}) async-start(), calls=%async_computation.22 | async-start | bytes 2408448 | tf_op jit(solution)/shard_map/all_gather | solution.py:214
  383.5 47.9 %all-gather.27.cloned.1.call-start = ((), (), s32[]{:S(2)}) async-start(), calls=%async_computation.23 | async-start | bytes 2408448 | tf_op jit(solution)/shard_map/all_gather | solution.py:279
  384.1 62.9 %reduce-scatter.25.cloned.1.call-start = ((), (), s32[]{:S(2)}) async-start(), calls=%async_computation.27 | async-start | bytes 2408448 | tf_op jit(solution)/shard_map/reduce_scatter | solution.py:225
  431.2 25.3 %reduce-scatter.21.cloned.1.call-start = ((), (), s32[]{:S(2)}) async-start(), calls=%async_computation.24 | async-start | bytes 2408448 | tf_op jit(solution)/shard_map/reduce_scatter | solution.py:293
  446.1 43.4 %all-gather.31.cloned.1.call-start = ((), (), s32[]{:S(2)}) async-start(), calls=%async_computation.28 | async-start | bytes 2408448 | tf_op jit(solution)/shard_map/all_gather | solution.py:172
  449.7 21.6 %collective-permute-start.2 = (bf16[98,8,512]{2,1,0:T(8,128)(2,1)}, bf16[98,8,512]{2,1,0:T(8,128)(2,1)}, u32[]{:S(2)}, u32[]{:S(2)}) collective-permute-start(bf16[98,8,512]{2,1,0:T(8,128)(2,1)} %add_convert_fusion.5), channel_id=1, source_target_pairs={{0,2},{1,3},{4,6},{5,7},{8,10},{9,11},{12,14},{13,15},{16,18},{17,... | collective-permute-start | bytes 2408456 | tf_op jit(solution)/shard_map/ppermute | solution.py:21
  476.6 55.2 %all-gather.29.cloned.1.call-start = ((), (), s32[]{:S(2)}) async-start(), calls=%async_computation.25 | async-start | bytes 2408448 | tf_op jit(solution)/shard_map/all_gather | solution.py:306
  477.3 199.1 %reduce-scatter.27.cloned.1.call-start = ((), (), s32[]{:S(2)}) async-start(), calls=%async_computation.29 | async-start | bytes 2408448 | tf_op jit(solution)/shard_map/reduce_scatter | solution.py:199
  608.3 78.4 %reduce-scatter.23.cloned.1.call-start = ((), (), s32[]{:S(2)}) async-start(), calls=%async_computation.26 | async-start | bytes 2408448 | tf_op jit(solution)/shard_map/reduce_scatter | solution.py:358
  676.3 49.0 %all-gather.33.cloned.1.call-start = ((), (), s32[]{:S(2)}) async-start(), calls=%async_computation.30 | async-start | bytes 2408448 | tf_op jit(solution)/shard_map/all_gather | solution.py:214
  696.4 61.6 %all-gather.35.cloned.1.call-start = ((), (), s32[]{:S(2)}) async-start(), calls=%async_computation.31 | async-start | bytes 2408448 | tf_op jit(solution)/shard_map/all_gather | solution.py:279
  701.0 22.3 %collective-permute-start.1 = (bf16[98,8,512]{2,1,0:T(8,128)(2,1)}, bf16[98,8,512]{2,1,0:T(8,128)(2,1)S(1)}, u32[]{:S(2)}, u32[]{:S(2)}) collective-permute-start(bf16[98,8,512]{2,1,0:T(8,128)(2,1)} %add_add_fusion.12), channel_id=1, source_target_pairs={{2,0},{3,1},{6,4},{7,5},{10,8},{11,9},{14,12},{15,13},{18,16},{19,... | collective-permute-start | bytes 2408456 | tf_op jit(solution)/shard_map/ppermute | solution.py:21
  725.2 56.0 %reduce-scatter.29.cloned.1.call-start = ((), (), s32[]{:S(2)}) async-start(), calls=%async_computation.32 | async-start | bytes 2408448 | tf_op jit(solution)/shard_map/reduce_scatter | solution.py:293
  770.8 39.7 %all-gather.37.cloned.1.call-start = ((), (), s32[]{:S(2)}) async-start(), calls=%async_computation.33 | async-start | bytes 2408448 | tf_op jit(solution)/shard_map/all_gather | solution.py:306
  788.1 113.1 %reduce-scatter.31.cloned.1.call-start = ((), (), s32[]{:S(2)}) async-start(), calls=%async_computation.34 | async-start | bytes 2408448 | tf_op jit(solution)/shard_map/reduce_scatter | solution.py:358
  891.6 52.9 %all-gather.39.cloned.1.call-start = ((), (), s32[]{:S(2)}) async-start(), calls=%async_computation.35 | async-start | bytes 2408448 | tf_op jit(solution)/shard_map/all_gather | solution.py:279
  908.0 23.0 %collective-permute-start.3 = (bf16[98,8,512]{2,1,0:T(8,128)(2,1)}, bf16[98,8,512]{2,1,0:T(8,128)(2,1)S(1)}, u32[]{:S(2)}, u32[]{:S(2)}) collective-permute-start(bf16[98,8,512]{2,1,0:T(8,128)(2,1)} %get-tuple-element.122), channel_id=1, source_target_pairs={{2,0},{3,1},{6,4},{7,5},{10,8},{11,9},{14,12},{15,13},{18,16},{19,... | collective-permute-start | bytes 2408456 | tf_op jit(solution)/shard_map/ppermute | solution.py:21
  932.9 36.5 %reduce-scatter.33.cloned.1.call-start = ((), (), s32[]{:S(2)}) async-start(), calls=%async_computation.36 | async-start | bytes 2408448 | tf_op jit(solution)/shard_map/reduce_scatter | solution.py:293
  959.1 27.9 %all-gather.41.cloned.1.call-start = ((), (), s32[]{:S(2)}) async-start(), calls=%async_computation.37 | async-start | bytes 2408448 | tf_op jit(solution)/shard_map/all_gather | solution.py:306
  975.8 207.3 %all-reduce.5.cloned.1.call-start = ((), (), s32[]{:S(2)}) async-start(), calls=%async_computation.42 | async-start | bytes 4194304
  1068.1 116.8 %reduce-scatter.35.cloned.1.call-start = ((), (), s32[]{:S(2)}) async-start(), calls=%async_computation.38 | async-start | bytes 2408448 | tf_op jit(solution)/shard_map/reduce_scatter | solution.py:358
  1077.5 177.6 %reduce-scatter.41.cloned.1.call-start = ((), (), s32[]{:S(2)}) async-start(), calls=%async_computation.41 | async-start | bytes 2359296 | tf_op jit(solution)/shard_map/reduce_scatter | solution.py:404
  1087.1 168.0 %reduce-scatter.39.cloned.1.call-start = ((), (), s32[]{:S(2)}) async-start(), calls=%async_computation.40 | async-start | bytes 2359296 | tf_op jit(solution)/shard_map/reduce_scatter | solution.py:403
  1094.1 224.0 %reduce-scatter.37.cloned.1.call-start = ((), (), s32[]{:S(2)}) async-start(), calls=%async_computation.39 | async-start | bytes 589824 | tf_op jit(solution)/shard_map/reduce_scatter | solution.py:402
  1102.9 82.0 %copy-start.110 = (f32[1,1,512]{2,1,0:T(1,128)S(1)}, f32[1,1,512]{2,1,0:T(1,128)}, u32[]{:S(2)}) copy-start(f32[1,1,512]{2,1,0:T(1,128)} %copy-done.108) | copy-start | bytes 6148
  1106.1 78.8 %copy-start.9 = (bf16[98,8,512]{2,1,0:T(8,128)(2,1)S(1)}, bf16[98,8,512]{2,1,0:T(8,128)(2,1)}, u32[]{:S(2)}) copy-start(bf16[98,8,512]{2,1,0:T(8,128)(2,1)} %copy-done.8) | copy-start | bytes 2408452
  1106.1 78.9 %copy-start.13 = (bf16[98,8,512]{2,1,0:T(8,128)(2,1)S(1)}, bf16[98,8,512]{2,1,0:T(8,128)(2,1)}, u32[]{:S(2)}) copy-start(bf16[98,8,512]{2,1,0:T(8,128)(2,1)} %copy-done.11) | copy-start | bytes 2408452
  1106.1 81.0 %copy-start.127 = (f32[512]{0:T(512)S(1)}, f32[512]{0:T(512)}, u32[]{:S(2)}) copy-start(f32[512]{0:T(512)} %get-tuple-element.87) | copy-start | bytes 6148
  1184.9 65.5 %copy-start.99 = (f32[1,1,512]{2,1,0:T(1,128)S(1)}, f32[1,1,512]{2,1,0:T(1,128)}, u32[]{:S(2)}) copy-start(f32[1,1,512]{2,1,0:T(1,128)} %copy-done.97) | copy-start | bytes 6148
  1184.9 65.5 %copy-start.101 = (f32[98,8]{1,0:T(8,128)S(1)}, f32[98,8]{1,0:T(8,128)}, u32[]{:S(2)}) copy-start(f32[98,8]{1,0:T(8,128)} %copy-done.100) | copy-start | bytes 9412
  1250.4 67.7 %copy-start.1 = (f32[1,8,169]{2,1,0:T(8,128)S(1)}, f32[1,8,169]{2,1,0:T(8,128)}, u32[]{:S(2)}) copy-start(f32[1,8,169]{2,1,0:T(8,128)} %param.18) | copy-start | bytes 16228
  (148 other events, 1206.4 us)
Sparse Core Ops, SparseCore 0:
  14.2 12.5 all-gather.14
  142.5 10.6 reduce-scatter.14
  258.3 7.6 reduce-scatter.16
  383.6 11.0 all-gather.24
  396.1 11.0 all-gather.26
  476.7 12.7 all-gather.30
  491.1 11.0 all-gather.28
  608.4 10.2 reduce-scatter.26
  676.4 10.2 reduce-scatter.22
  788.2 10.1 all-gather.36
  891.7 9.4 reduce-scatter.30
  975.9 11.0 all-gather.40
  1077.6 10.2 reduce-scatter.34
  1091.8 90.5 reduce-scatter.40
  1186.3 67.1 reduce-scatter.38
  1257.3 60.7 reduce-scatter.36
Sparse Core Ops, SparseCore 1:
  145.0 41.9 all-gather.18
  188.9 8.2 all-gather.16
  199.2 41.6 all-gather.20
  291.0 11.6 all-gather.22
  365.4 10.2 reduce-scatter.18
  431.2 10.2 reduce-scatter.24
  446.2 10.2 reduce-scatter.20
  696.5 10.9 all-gather.32
  725.3 10.0 all-gather.34
  770.9 9.4 reduce-scatter.28
  933.0 11.4 all-gather.38
  959.2 10.2 reduce-scatter.32
  1068.2 114.9 all-reduce.4
where the time goes:
time: 1330 us
  matrix products  345 us (26%)
  waiting for transfers between devices  320 us (24%)
  local copies, waits for them, and re-layouts  313 us (24%)
  blocking collectives  163 us (12%)
  other arithmetic  152 us (11%)
  between operations  19.8 us (1%)
    reduce_scatter x1, waiting for transfers between devices, on_device(): lax.psum_scatter(matrix_parts[1], 'dp', scatter_dimension=0, tiled=True)  62.9 us
    psum x1, blocking collectives, on_device(): lax.psum((shared_total[0], shared_total[1], shared_total[2]), ('dp', 'ten...  59.9 us
    dot_general x3, matrix products, on_device(): jnp.einsum('sbd,df->sbf', forward_normed_two_full, fc1_weight, preferred_...  57.5 us
    ppermute x4, waiting for transfers between devices, passed_along(): return lax.ppermute(array, axis, pairs)  48.3 us
    concatenate x9, local copies, waits for them, and re-layouts, on_device(): jnp.concatenate([grad_query.reshape(windows_n, WIN * WIN, qkv_width), gra...  47 us
    unnamed x30, waiting for transfers between devices  40.1 us
    psum x1, blocking collectives, on_device(): head_sum = lax.psum((head_total[0], head_total[1], head_total[2]), 'dp')  38.7 us
    all_gather x1, waiting for transfers between devices, on_device(): lax.all_gather(w_fc2, 'dp', axis=1, tiled=True)  37.4 us
  transfers between devices with their start and end apart: 33, of which 21 were waited for; matrix products, arithmetic and copies ran while one was open for 26% of the time, Pallas kernels for 0%

commit v1 on v0

v1 whole, which is shorter than its diff:
```python
from functools import partial

import jax
import jax.numpy as jnp
import numpy as np
from jax import lax
from jax.experimental import pallas as pl
from jax.experimental.pallas import tpu as pltpu
from jax.sharding import PartitionSpec as P

D = 512
HEADS = 16
HD = 32
FF = 2048
SIDE = 14
WIN = 7
SHIFT = 3
NW = 4
WP = 64
IMG_ROWS = NW * WP
GH = 4
NG = HEADS // GH
Q_SCALE = HD ** (-0.5)
TABLE = (2 * WIN - 1) ** 2
F32 = jnp.float32
BF16 = jnp.bfloat16
HIGHEST = lax.Precision.HIGHEST
ALL_AXES = ("dp", "tensor", "pipe")


def token_order(offset):
    order = np.full((IMG_ROWS,), -1, np.int64)
    per_side = SIDE // WIN
    for win in range(NW):
        for place in range(WIN * WIN):
            row = (win // per_side) * WIN + place // WIN
            col = (win % per_side) * WIN + place % WIN
            order[win * WP + place] = ((row + offset) % SIDE) * SIDE + (col + offset) % SIDE
    return order


def one_hot_order(offset):
    order = token_order(offset)
    return (order[:, None] == np.arange(SIDE * SIDE)[None, :]).astype(np.float32)


def rel_one_hot():
    places = np.arange(WP)
    rows_in, cols_in = places // WIN, places % WIN
    index = (rows_in[None, :] - rows_in[:, None] + WIN - 1) * (2 * WIN - 1) + (
        cols_in[None, :] - cols_in[:, None] + WIN - 1
    )
    real = places < WIN * WIN
    index = np.where(real[:, None] & real[None, :], index, -1).astype(np.int32)
    return (jnp.asarray(index)[None] == jnp.arange(TABLE, dtype=jnp.int32)[:, None, None]).astype(F32)


def region_masks():
    def region(pos):
        return (pos >= SIDE - WIN).astype(np.int64) + (pos >= SIDE - SHIFT).astype(np.int64)

    per_side = SIDE // WIN
    out = np.zeros((NW, WP, WP), np.float32)
    places = np.arange(WIN * WIN)
    for win in range(NW):
        row = (win // per_side) * WIN + places // WIN
        col = (win % per_side) * WIN + places % WIN
        label = 3 * region(row) + region(col)
        out[win, : WIN * WIN, : WIN * WIN] = np.where(label[:, None] != label[None, :], -100.0, 0.0)
    return out


def score_bias(table, mask):
    hot = rel_one_hot().reshape(TABLE, WP * WP)
    bias = jnp.dot(table, hot, precision=HIGHEST).reshape(NG, GH, WP, WP)
    pad = jnp.where(jnp.arange(WP) >= WIN * WIN, -1e30, 0.0).astype(F32)
    bias = bias.transpose(0, 2, 1, 3)[None] + pad[None, None, :, None, None]
    bias = bias + jnp.asarray(mask)[:, None, :, None, :]
    return bias.reshape(mask.shape[0], NG, WP, GH * WP)


def dot(a, b, a_dim, b_dim):
    return lax.dot_general(a, b, (((a_dim,), (b_dim,)), ((), ())), preferred_element_type=F32)


def normalize(values):
    center = values - jnp.mean(values, axis=-1, keepdims=True)
    spread = jnp.mean(center * center, axis=-1, keepdims=True)
    rstd = lax.rsqrt(spread + 1e-05)
    return center * rstd, rstd


def norm_back(grad, n, rstd, gain):
    e = grad * gain
    return rstd * (
        e - jnp.mean(e, axis=-1, keepdims=True) - n * jnp.mean(e * n, axis=-1, keepdims=True)
    )


def spread_heads(block):
    lane_head = lax.broadcasted_iota(jnp.int32, block.shape, 1) // HD
    wide = block.astype(F32)
    return jnp.concatenate(
        [jnp.where(lane_head == h, wide, 0.0).astype(BF16) for h in range(GH)], axis=0
    )


def fold_heads(block):
    lane_head = lax.broadcasted_iota(jnp.int32, (WP, GH * HD), 1) // HD
    out = jnp.zeros((WP, GH * HD), F32)
    for h in range(GH):
        out = jnp.where(lane_head == h, block[h * WP : (h + 1) * WP], out)
    return out


def softmax_rows(scores):
    top = jnp.max(scores, axis=0, keepdims=True)
    part = jnp.exp(scores - top)
    return part / jnp.sum(part, axis=0, keepdims=True)


def attend(bias_ref, qkv_s, o_s, p_s):
    wins = bias_ref.shape[0]

    def one_window(win, carry):
        rows = pl.ds(pl.multiple_of(win * WP, WP), WP)
        for g in range(NG):
            lanes = slice(g * 128, (g + 1) * 128)
            q = qkv_s[rows, lanes]
            k = qkv_s[rows, D + g * 128 : D + (g + 1) * 128]
            v = qkv_s[rows, 2 * D + g * 128 : 2 * D + (g + 1) * 128]
            bias = bias_ref[win, g] if wins > 1 else bias_ref[0, g]
            p = softmax_rows(dot(k, spread_heads(q), 1, 1) + bias)
            if p_s is not None:
                p_s[win, g] = p
            o_s[rows, lanes] = fold_heads(dot(p.astype(BF16), v, 0, 0)).astype(BF16)
        return carry

    lax.fori_loop(0, NW, one_window, 0)


def attend_back(qkv_s, do_s, p_s, dqkv_ref, base, table_ref):
    def one_window(win, carry):
        rows = pl.ds(pl.multiple_of(win * WP, WP), WP)
        out_rows = pl.ds(pl.multiple_of(base + win * WP, WP), WP)
        for g in range(NG):
            lanes = slice(g * 128, (g + 1) * 128)
            k_lanes = slice(D + g * 128, D + (g + 1) * 128)
            v_lanes = slice(2 * D + g * 128, 2 * D + (g + 1) * 128)
            q_wide = spread_heads(qkv_s[rows, lanes])
            do_wide = spread_heads(do_s[rows, lanes])
            k = qkv_s[rows, k_lanes]
            v = qkv_s[rows, v_lanes]
            p = p_s[win, g]
            dp = dot(v, do_wide, 1, 1)
            ds = (p * (dp - jnp.sum(p * dp, axis=0, keepdims=True))).astype(BF16)
            table_ref[g] += ds.astype(F32)
            dqkv_ref[out_rows, lanes] = (fold_heads(dot(ds, k, 0, 0)) * Q_SCALE).astype(BF16)
            dqkv_ref[out_rows, k_lanes] = dot(ds, q_wide, 1, 0).astype(BF16)
            dqkv_ref[out_rows, v_lanes] = dot(p.astype(BF16), do_wide, 1, 0).astype(BF16)
        return carry

    lax.fori_loop(0, NW, one_window, 0)


def forward_half(x, small_ref, wqkv_ref, wproj_ref, bias_ref, qkv_s, o_s, p_s):
    n1, r1 = normalize(x)
    h = (n1 * small_ref[0:1] + small_ref[1:2]).astype(BF16)
    qkv_s[:, 0:D] = ((dot(h, wqkv_ref[0], 1, 0) + small_ref[4:5]) * Q_SCALE).astype(BF16)
    qkv_s[:, D : 2 * D] = dot(h, wqkv_ref[1], 1, 0).astype(BF16)
    qkv_s[:, 2 * D : 3 * D] = (dot(h, wqkv_ref[2], 1, 0) + small_ref[5:6]).astype(BF16)
    attend(bias_ref, qkv_s, o_s, p_s)
    o = o_s[...]
    x1 = x + (dot(o, wproj_ref[...], 1, 1) + small_ref[6:7])
    n2, r2 = normalize(x1)
    h2 = (n2 * small_ref[2:3] + small_ref[3:4]).astype(BF16)
    return n1, r1, h, o, x1, n2, r2, h2


def gelu_parts(u):
    cdf = 0.5 * (1.0 + lax.erf(u * np.float32(0.5**0.5)))
    return cdf


def fwd_kernel(x_ref, small_ref, fc1b_ref, wqkv_ref, wproj_ref, wfc1_ref, wfc2_ref, bias_ref,
               y_ref, qkv_s, o_s):
    def one_image(img, carry):
        x = x_ref[img].astype(F32)
        parts = forward_half(x, small_ref, wqkv_ref, wproj_ref, bias_ref, qkv_s, o_s, None)
        x1, h2 = parts[4], parts[7]
        total = x1 + small_ref[7:8]
        for c in range(FF // 512):
            cols = slice(c * 512, (c + 1) * 512)
            u = dot(h2, wfc1_ref[:, cols], 1, 0) + fc1b_ref[0:1, cols]
            a = (u * gelu_parts(u)).astype(BF16)
            total = total + dot(a, wfc2_ref[:, cols], 1, 1)
        y_ref[img] = total.astype(BF16)
        return carry

    lax.fori_loop(0, x_ref.shape[0], one_image, 0)


def bwd_kernel(x_ref, g_ref, small_ref, fc1b_ref, wqkv_ref, wproj_ref, wfc1_ref, wfc2_ref, bias_ref,
               dx_ref, gqkv_ref, gproj_ref, gfc1_ref, gfc2_ref, gsmall_ref, gfc1b_ref, gtable_ref,
               qkv_s, o_s, p_s, do_s, h_all, o_all, h2_all, dz_all, dy_all, a_all, du_all, dqkv_all):
    gsmall_ref[...] = jnp.zeros_like(gsmall_ref)
    gfc1b_ref[...] = jnp.zeros_like(gfc1b_ref)
    gtable_ref[...] = jnp.zeros_like(gtable_ref)

    def add_row(row, values):
        gsmall_ref[row : row + 1] += jnp.sum(values, axis=0, keepdims=True)

    def one_image(img, carry):
        base = pl.multiple_of(img * IMG_ROWS, IMG_ROWS)
        rows = pl.ds(base, IMG_ROWS)
        x = x_ref[img].astype(F32)
        n1, r1, h, o, x1, n2, r2, h2 = forward_half(
            x, small_ref, wqkv_ref, wproj_ref, bias_ref, qkv_s, o_s, p_s
        )
        h_all[rows] = h
        o_all[rows] = o
        h2_all[rows] = h2
        dz = g_ref[img]
        dz_all[rows] = dz
        g_out = dz.astype(F32)
        add_row(7, g_out)
        dh2 = jnp.zeros((IMG_ROWS, D), F32)
        for c in range(FF // 512):
            cols = slice(c * 512, (c + 1) * 512)
            u = dot(h2, wfc1_ref[:, cols], 1, 0) + fc1b_ref[0:1, cols]
            cdf = gelu_parts(u)
            a_all[rows, cols] = (u * cdf).astype(BF16)
            pdf = jnp.exp(-0.5 * u * u) * np.float32((2.0 * np.pi) ** -0.5)
            du = ((cdf + u * pdf) * dot(dz, wfc2_ref[:, cols], 1, 0)).astype(BF16)
            du_all[rows, cols] = du
            gfc1b_ref[0:1, cols] += jnp.sum(du.astype(F32), axis=0, keepdims=True)
            dh2 = dh2 + dot(du, wfc1_ref[:, cols], 1, 1)
        add_row(2, dh2 * n2)
        add_row(3, dh2)
        dx1 = g_out + norm_back(dh2, n2, r2, small_ref[2:3])
        dy = dx1.astype(BF16)
        dy_all[rows] = dy
        add_row(6, dy.astype(F32))
        do_s[...] = dot(dy, wproj_ref[...], 1, 0).astype(BF16)
        attend_back(qkv_s, do_s, p_s, dqkv_all, base, gtable_ref)
        dq = dqkv_all[rows, 0:D]
        dk = dqkv_all[rows, D : 2 * D]
        dv = dqkv_all[rows, 2 * D : 3 * D]
        add_row(4, dq.astype(F32))
        add_row(5, dv.astype(F32))
        dh = dot(dq, wqkv_ref[0], 1, 1) + dot(dk, wqkv_ref[1], 1, 1) + dot(dv, wqkv_ref[2], 1, 1)
        add_row(0, dh * n1)
        add_row(1, dh)
        dx_ref[img] = (dx1 + norm_back(dh, n1, r1, small_ref[0:1])).astype(BF16)
        return carry

    lax.fori_loop(0, x_ref.shape[0], one_image, 0)
    for c in range(3):
        gqkv_ref[c] = dot(h_all[...], dqkv_all[:, c * D : (c + 1) * D], 0, 0).astype(BF16)
    gproj_ref[...] = dot(dy_all[...], o_all[...], 0, 0).astype(BF16)
    for c in range(FF // 512):
        cols = slice(c * 512, (c + 1) * 512)
        gfc1_ref[:, cols] = dot(h2_all[...], du_all[:, cols], 0, 0).astype(BF16)
        gfc2_ref[:, cols] = dot(dz_all[...], a_all[:, cols], 0, 0).astype(BF16)


VMEM = pl.BlockSpec(memory_space=pltpu.VMEM)


def layer_cost(images, passes):
    tokens = images * IMG_ROWS
    return pl.CostEstimate(
        flops=passes * tokens * 2 * (4 * D * D + 2 * D * FF),
        bytes_accessed=20_000_000,
        transcendentals=tokens * (FF + HEADS * WP),
    )


def run_forward(x, small, fc1b, mats, bias):
    images = x.shape[0]
    return pl.pallas_call(
        fwd_kernel,
        out_shape=jax.ShapeDtypeStruct(x.shape, BF16),
        in_specs=[VMEM] * 8,
        out_specs=VMEM,
        scratch_shapes=[pltpu.VMEM((IMG_ROWS, 3 * D), BF16), pltpu.VMEM((IMG_ROWS, D), BF16)],
        compiler_params=pltpu.CompilerParams(vmem_limit_bytes=40 * 1024 * 1024),
        cost_estimate=layer_cost(images, 3),
    )(x, small, fc1b, *mats, bias)


def run_backward(x, grad, small, fc1b, mats, bias):
    images = x.shape[0]
    tokens = images * IMG_ROWS
    shape = jax.ShapeDtypeStruct
    return pl.pallas_call(
        bwd_kernel,
        out_shape=[
            shape(x.shape, BF16),
            shape((3, D, D), BF16),
            shape((D, D), BF16),
            shape((D, FF), BF16),
            shape((D, FF), BF16),
            shape((8, D), F32),
            shape((1, FF), F32),
            shape((NG, WP, GH * WP), F32),
        ],
        in_specs=[VMEM] * 9,
        out_specs=[VMEM] * 8,
        scratch_shapes=[
            pltpu.VMEM((IMG_ROWS, 3 * D), BF16),
            pltpu.VMEM((IMG_ROWS, D), BF16),
            pltpu.VMEM((NW, NG, WP, GH * WP), F32),
            pltpu.VMEM((IMG_ROWS, D), BF16),
            pltpu.VMEM((tokens, D), BF16),
            pltpu.VMEM((tokens, D), BF16),
            pltpu.VMEM((tokens, D), BF16),
            pltpu.VMEM((tokens, D), BF16),
            pltpu.VMEM((tokens, D), BF16),
            pltpu.VMEM((tokens, FF), BF16),
            pltpu.VMEM((tokens, FF), BF16),
            pltpu.VMEM((tokens, 3 * D), BF16),
        ],
        compiler_params=pltpu.CompilerParams(vmem_limit_bytes=56 * 1024 * 1024),
        cost_estimate=layer_cost(images, 9),
    )(x, grad, small, fc1b, *mats, bias)


def pack_shard(qkv, proj, fc1, fc2):
    rows, cols = proj.shape
    def quarters(m):
        return m.reshape(rows, FF // D, cols).transpose(1, 0, 2).reshape(-1, cols)
    return jnp.concatenate([qkv.reshape(-1, cols), proj, quarters(fc1), quarters(fc2)], axis=0)


def unpack_shard(packed, rows, cols):
    def wide(m):
        return m.reshape(FF // D, rows, cols).transpose(1, 0, 2).reshape(rows, FF // D * cols)
    return (
        packed[: 3 * rows].reshape(3, rows, cols),
        packed[3 * rows : 4 * rows],
        wide(packed[4 * rows : 8 * rows]),
        wide(packed[8 * rows :]),
    )


def unpack_full(gathered, dp, tensor, rows, cols):
    parts = gathered.reshape(dp, tensor, 12, rows, cols)
    qkv = parts[:, :, 0:3].transpose(2, 0, 3, 1, 4).reshape(3, D, D)
    proj = parts[:, :, 3].transpose(0, 2, 1, 3).reshape(D, D)
    fc1 = parts[:, :, 4:8].transpose(0, 3, 1, 2, 4).reshape(D, FF)
    fc2 = parts[:, :, 8:12].transpose(0, 3, 1, 2, 4).reshape(D, FF)
    return qkv, proj, fc1, fc2


def pack_full(qkv, proj, fc1, fc2, dp, tensor, rows, cols):
    q = qkv.reshape(3, dp, rows, tensor, cols).transpose(1, 3, 0, 2, 4)
    p = proj.reshape(1, dp, rows, tensor, cols).transpose(1, 3, 0, 2, 4)
    f1 = fc1.reshape(dp, rows, tensor, FF // D, cols).transpose(0, 2, 3, 1, 4)
    f2 = fc2.reshape(dp, rows, tensor, FF // D, cols).transpose(0, 2, 3, 1, 4)
    return jnp.concatenate([q, p, f1, f2], axis=2).reshape(-1, cols)


def swapped(array, axis):
    return lax.ppermute(array, axis, [(0, 1), (1, 0)])


def half_of(array, which, axis):
    size = array.shape[axis] // 2
    return lax.dynamic_slice_in_dim(array, which * size, size, axis)


def on_device(ends, image_counts, norm_gains, norm_shifts, w_qkv, qv_bias, rel_table, w_proj,
              out_biases, w_fc1, fc1_bias, w_fc2):
    pipe = lax.axis_index("pipe")
    tensor = lax.axis_index("tensor")
    first = pipe == 0
    dp_n, tensor_n = lax.axis_size("dp"), lax.axis_size("tensor")
    rows, cols = w_proj.shape[1], w_proj.shape[2]

    shard = pack_shard(w_qkv[0], w_proj[0], w_fc1[0], w_fc2[0])
    kept = half_of(shard, pipe, 0)
    got = swapped(half_of(shard, 1 - pipe, 0), "pipe")
    gathered = [
        lax.all_gather(jnp.where(first, kept, got), ALL_AXES, axis=0, tiled=True),
        lax.all_gather(jnp.where(first, got, kept), ALL_AXES, axis=0, tiled=True),
    ]
    mats = [unpack_full(g, dp_n, tensor_n, rows, cols) for g in gathered]

    heads_here = rel_table.shape[1]
    sizes = (2 * D, 2 * D, 2 * D, 2 * cols, fc1_bias.shape[1], heads_here * TABLE)
    small_local = jnp.concatenate(
        [a.reshape(-1) for a in (norm_gains, norm_shifts, out_biases, qv_bias, fc1_bias, rel_table)]
    )
    small_all = lax.all_gather(small_local, ("pipe", "tensor"), axis=0, tiled=True).reshape(2, 2, -1)
    cuts = np.cumsum((0,) + sizes)
    smalls, hidden, biases = [], [], []
    region = region_masks()
    for layer in range(2):
        mine = [small_all[layer, :, cuts[i] : cuts[i + 1]] for i in range(6)]
        gains = mine[0][0].reshape(2, D)
        shifts = mine[1][0].reshape(2, D)
        outs = mine[2][0].reshape(2, D)
        qv = mine[3].reshape(2, 2, cols).transpose(1, 0, 2).reshape(2, D)
        smalls.append(
            jnp.concatenate(
                [gains[0:1], shifts[0:1], gains[1:2], shifts[1:2], qv[0:1], qv[1:2], outs], axis=0
            )
        )
        hidden.append(mine[4].reshape(1, FF))
        table = mine[5].reshape(HEADS, TABLE)
        biases.append(score_bias(table, region if layer == 1 else region[:1] * 0.0))

    own = ends[0]
    got_rows = swapped(half_of(own, 1 - pipe, 1), "pipe")
    kept_rows = half_of(own, pipe, 1)
    both = jnp.stack([jnp.where(first, kept_rows, got_rows), jnp.where(first, got_rows, kept_rows)])

    def whole_images(part):
        mine = half_of(part, tensor, 1)
        other = swapped(half_of(part, 1 - tensor, 1), "tensor")
        return jnp.concatenate(
            [jnp.where(tensor == 0, mine, other), jnp.where(tensor == 0, other, mine)], axis=0
        )

    x_tokens, c_tokens = whole_images(both[0]), whole_images(both[1])
    images = x_tokens.shape[1]
    slots = (pipe * 2 + tensor) * images + jnp.arange(images, dtype=jnp.int32)
    real = (slots < image_counts[0]).astype(BF16)
    c_tokens = c_tokens * real[None, :, None]
    order = [one_hot_order(0), one_hot_order(SHIFT)]

    def placed(matrix, tokens, spec):
        return jnp.einsum(spec, jnp.asarray(matrix, BF16), tokens, preferred_element_type=F32).astype(BF16)

    x_in = placed(order[0], x_tokens, "rs,sbd->brd")
    c_in = placed(order[1], c_tokens, "rs,sbd->brd")

    y0 = run_forward(x_in, smalls[0], hidden[0], mats[0], biases[0])
    y0 = placed(order[1] @ order[0].T, y0, "rs,bsd->brd")
    back1 = run_backward(y0, c_in, smalls[1], hidden[1], mats[1], biases[1])
    g_mid = placed(order[0] @ order[1].T, back1[0], "rs,bsd->brd")
    g1 = lax.psum_scatter(
        pack_full(*back1[1:5], dp_n, tensor_n, rows, cols), ALL_AXES, scatter_dimension=0, tiled=True
    )
    back0 = run_backward(x_in, g_mid, smalls[0], hidden[0], mats[0], biases[0])
    g0 = lax.psum_scatter(
        pack_full(*back0[1:5], dp_n, tensor_n, rows, cols), ALL_AXES, scatter_dimension=0, tiled=True
    )

    other = swapped(jnp.where(first, g1, g0), "pipe")
    mine = jnp.where(first, g0, g1)
    mats_grad = jnp.where(
        first, jnp.concatenate([mine, other], axis=0), jnp.concatenate([other, mine], axis=0)
    ).astype(F32)
    qkv_g, proj_g, fc1_g, fc2_g = unpack_shard(mats_grad, rows, cols)

    hot = rel_one_hot().reshape(TABLE, WP * WP)

    def small_grads(back):
        scores = back[7].reshape(NG, WP, GH, WP).transpose(0, 2, 1, 3).reshape(HEADS, WP * WP)
        table = lax.dot_general(scores, hot, (((1,), (1,)), ((), ())), precision=HIGHEST)
        return jnp.concatenate([back[5].reshape(-1), back[6].reshape(-1), table.reshape(-1)])

    summed = lax.psum(jnp.stack([small_grads(back0), small_grads(back1)]), ALL_AXES)
    summed = jnp.where(first, summed[0], summed[1])
    rows_g = summed[: 8 * D].reshape(8, D)
    gains_g = jnp.stack([rows_g[0], rows_g[2]])
    shifts_g = jnp.stack([rows_g[1], rows_g[3]])
    qv_g = half_of(rows_g[4:6], tensor, 1)
    outs_g = rows_g[6:8]
    fc1b_g = half_of(summed[8 * D : 8 * D + FF], tensor, 0)
    table_g = half_of(summed[8 * D + FF :].reshape(HEADS, TABLE), tensor, 0)

    dx = placed(order[0], back0[0], "rs,brd->sbd")
    gm = placed(order[0], g_mid, "rs,brd->sbd")

    def split_rows(tokens):
        mine = half_of(tokens, tensor, 0)
        other = swapped(half_of(tokens, 1 - tensor, 0), "tensor")
        return jnp.concatenate(
            [jnp.where(tensor == 0, mine, other), jnp.where(tensor == 0, other, mine)], axis=1
        )

    dx, gm = split_rows(dx), split_rows(gm)
    other = swapped(jnp.where(first, gm, dx), "pipe")
    mine = jnp.where(first, dx, gm)
    section = jnp.where(
        first, jnp.concatenate([mine, other], axis=1), jnp.concatenate([other, mine], axis=1)
    )
    return (
        section[None],
        gains_g[None],
        shifts_g[None],
        qkv_g[None],
        qv_g[None],
        table_g[None],
        proj_g[None],
        outs_g[None],
        fc1_g[None],
        fc1b_g[None],
        fc2_g[None],
    )


def solution(mesh):
    return jax.shard_map(
        on_device,
        mesh=mesh,
        in_specs=(
            P("pipe", "tensor", "dp", None),
            P("dp"),
            P("pipe", None, None),
            P("pipe", None, None),
            P("pipe", None, "dp", "tensor"),
            P("pipe", None, "tensor"),
            P("pipe", "tensor", None),
            P("pipe", "dp", "tensor"),
            P("pipe", None, None),
            P("pipe", "dp", "tensor"),
            P("pipe", "tensor"),
            P("pipe", "dp", "tensor"),
        ),
        out_specs=(
            P("pipe", "tensor", "dp", None),
            P("pipe", None, None),
            P("pipe", None, None),
            P("pipe", None, "dp", "tensor"),
            P("pipe", None, "tensor"),
            P("pipe", "tensor", None),
            P("pipe", "dp", "tensor"),
            P("pipe", None, None),
            P("pipe", "dp", "tensor"),
            P("pipe", "tensor"),
            P("pipe", "dp", "tensor"),
        ),
        check_vma=False,
    )
```

time: 1330 us -> 792 us (0.60)
  matrix products: 345 us -> 20.3 us
  local copies, waits for them, and re-layouts: 313 us -> 150 us
  blocking collectives: 163 us -> 0 us
  Pallas kernels: 0 us -> 144 us
  other arithmetic: 152 us -> 26.5 us
  waiting for transfers between devices: 320 us -> 412 us
    dot_general x60 -> x10, matrix products: 345 us -> 20.3 us  [the longest x6 10 us: placed(): jnp.einsum(spec, jnp.asarray(matrix, BF16), tokens, preferred_element_typ...]
    pallas_call x0 -> x3, Pallas kernels: none -> 144 us  [the longest x2 121 us: run_backward(): pl.pallas_call(bwd_kernel, out_shape=[shape(x.shape, BF16), shape((3, D,...]
    reduce_scatter x14 -> x2, waiting for transfers between devices: 107 us -> 234 us  [the longest x1 119 us: on_device(): lax.psum_scatter(pack_full(*back0[1:5], dp_n, tensor_n, rows, cols), ALL_...]
    psum x2 -> x0, blocking collectives: 98.6 us -> none  [the longest x1 59.9 us: on_device(): lax.psum((shared_total[0], shared_total[1], shared_total[2]), ('dp', 'ten...]
    convert_element_type x12 -> x0, local copies, waits for them, and re-layouts: 87.1 us -> none  [the longest x3 21.9 us: on_device(): grad_query = (jnp.einsum('whqk,wkhe->wqhe', grad_scores, backward_key_w,...]
    reduce_sum x37 -> x0, other arithmetic: 84.9 us -> none  [the longest x10 19.9 us: layer_norm(): center = values - jnp.mean(values, axis=-1, keepdims=True)]
    all_gather x2 -> x0, blocking collectives: 64.3 us -> none  [the longest x1 32.6 us: on_device(): lax.all_gather(w_proj, 'dp', axis=1, tiled=True)]
    psum x0 -> x1, waiting for transfers between devices: none -> 64 us  [on_device(): lax.psum(jnp.stack([small_grads(back0), small_grads(back1)]), ALL_AXES)]
  transfers between devices with their start and end apart: 33 -> 14, of which waited for: 21 -> 8; matrix products, arithmetic and copies ran while one was open for 26% -> 12% of each run, Pallas kernels for 0% -> 0%
where the time goes in v1:
time: 792 us; the launch traced here: 781 us
  waiting for transfers between devices  412 us (52%)
  local copies, waits for them, and re-layouts  150 us (19%)
  Pallas kernels  144 us (18%)
  other arithmetic  26.5 us (3%)
  matrix products  20.3 us (3%)
  between operations  18.2 us (2%)
  starting transfers between devices  9.2 us (1%)
    pallas_call x2, Pallas kernels, run_backward(): pl.pallas_call(bwd_kernel, out_shape=[shape(x.shape, BF16), shape((3, D,...  121 us
    reduce_scatter x1, waiting for transfers between devices, on_device(): lax.psum_scatter(pack_full(*back0[1:5], dp_n, tensor_n, rows, cols), ALL_...  119 us
    reduce_scatter x1, waiting for transfers between devices, on_device(): lax.psum_scatter(pack_full(*back1[1:5], dp_n, tensor_n, rows, cols), ALL_...  115 us
    psum x1, waiting for transfers between devices, on_device(): lax.psum(jnp.stack([small_grads(back0), small_grads(back1)]), ALL_AXES)  64 us
    all_gather x1, waiting for transfers between devices, on_device(): lax.all_gather(jnp.where(first, got, kept), ALL_AXES, axis=0, tiled=True)  63.8 us
    unnamed x7, waiting for transfers between devices  25.2 us
    pallas_call x1, Pallas kernels, run_forward(): pl.pallas_call(fwd_kernel, out_shape=jax.ShapeDtypeStruct(x.shape, BF16),...  23.5 us
    all_gather x1, waiting for transfers between devices, on_device(): lax.all_gather(jnp.where(first, kept, got), ALL_AXES, axis=0, tiled=True)  22.7 us
  transfers between devices with their start and end apart: 14, of which 8 were waited for; matrix products, arithmetic and copies ran while one was open for 12% of the time, Pallas kernels for 0%

profile of v1, /device:TPU:0, one launch (start us, length us, event | category | flops | bytes accessed | tf_op | source)
XLA Modules:
  0.0 781.0 jit_solution(17814249696045233980)
XLA Ops:
  11.3 3.0 collective-permute-start.2
  17.0 2.2 collective-permute-done.2
  24.6 24.6 %all-reduce.6.cloned.1.call-done = f32[23840]{0:T(1024)} async-done(((f32[23840]{0:T(1024)}), f32[23840]{0:T(1024)}) %all-reduce.6.cloned.1.call-update) | async-done | bytes 95376
  50.4 3.3 fusion.18
  54.2 3.3 fusion.24
  59.4 2.0 bitcast_select_fusion
  69.5 22.7 %all-gather.3.cloned.1.call-done = bf16[12288,256]{1,0:T(8,128)(2,1)} async-done(((bf16[384,256]{1,0:T(8,128)(2,1)}), bf16[12288,256]{1,0:T(8,128)(2,1)}) %all-gather.3.cloned.1.call-update) | async-done | bytes 6291472 | tf_op jit(solution)/shard_map/all_gather | solution.py:385
  92.2 2.7 slice.286
  96.0 4.0 fusion.40
  99.9 63.8 %all-gather.5.cloned.1.call-done = bf16[12288,256]{1,0:T(8,128)(2,1)} async-done(((bf16[384,256]{1,0:T(8,128)(2,1)}), bf16[12288,256]{1,0:T(8,128)(2,1)}) %all-gather.5.cloned.1.call-update) | async-done | bytes 6291472 | tf_op jit(solution)/shard_map/all_gather | solution.py:386
  163.8 4.8 fusion.39
  168.6 2.9 slice.300
  172.5 4.5 copy_bitcast_fusion.2
  177.0 3.3 reshape.401.wfc1_ref
  180.3 4.9 reshape.402.wfc2_ref
  185.2 4.3 copy.178
  189.4 3.7 reshape.399.wqkv_ref
  194.7 5.7 copy_bitcast_fusion
  200.4 4.5 reshape.407.wfc1_ref
  204.9 4.5 reshape.408.wfc2_ref
  209.4 4.2 copy.177
  213.6 3.8 reshape.405.wqkv_ref
  221.6 23.5 %shard_map.302 = bf16[4,256,512]{2,1,0:T(8,128)(2,1)S(1)} custom-call(bf16[4,256,512]{2,1,0:T(8,128)(2,1)S(1)} %copy-done.7, f32[8,512]{1,0:T(8,128)S(1)} %concatenate.86.small_ref, f32[1,2048]{1,0:T(1,128)S(1)} %bitcast.206, bf16[3,512,512]{2,1,0:T(8,128)(2,1)S(1)} %copy-done.2, bf16[512,512]{1,0:T(8,128)(2,1)S(1)} %bitcast.204, ...), custom_call_target="tpu_custom_call" | custom-call | flops 19327352832 | bytes 20000000 | tf_op jit(solution)/shard_map/pallas_call | solution.py:281
  246.6 60.4 %shard_map.303 = (bf16[4,256,512]{2,1,0:T(8,128)(2,1)}, bf16[3,512,512]{2,1,0:T(8,128)(2,1)}, bf16[512,512]{1,0:T(8,128)(2,1)}, bf16[512,2048]{1,0:T(8,128)(2,1)...) custom-call(bf16[4,256,512]{2,1,0:T(8,128)(2,1)} %fusion.13.x_ref, ...), custom_call_target="tpu_custom_call" | custom-call | flops 57982058496 | bytes 20000000 | tf_op jit(solution)/shard_map/pallas_call | solution.py:296
  306.9 3.7 reshape.424
  310.7 3.6 copy.175
  314.3 4.5 reshape.426
  318.8 4.6 reshape.427
  323.4 3.4 reshape.447
  326.8 2.7 fusion.14.g_ref
  329.4 60.4 %shard_map.304 = (bf16[4,256,512]{2,1,0:T(8,128)(2,1)}, bf16[3,512,512]{2,1,0:T(8,128)(2,1)}, bf16[512,512]{1,0:T(8,128)(2,1)}, bf16[512,2048]{1,0:T(8,128)(2,1)...) custom-call(bf16[4,256,512]{2,1,0:T(8,128)(2,1)} %fusion.11.x_ref, ...), custom_call_target="tpu_custom_call" | custom-call | flops 57982058496 | bytes 20000000 | tf_op jit(solution)/shard_map/pallas_call | solution.py:296
  389.9 2.0 reshape.411
  391.9 1.9 copy.181
  393.8 1.9 reshape.412
  395.8 2.4 fusion.6
  399.4 1.9 copy.180
  404.9 7.7 pad_maximum_fusion.1
  412.6 6.5 copy.124
  420.5 1.8 reshape.419
  422.4 3.6 copy.176
  426.0 4.6 reshape.421
  430.5 4.5 reshape.422
  435.1 3.4 reshape.446
  438.5 7.8 pad_maximum_fusion
  446.2 6.5 copy.121
  457.4 64.0 %all-reduce.4.cloned.1.call-done = f32[2,8848]{1,0:T(2,128)} async-done(((f32[2,8848]{1,0:T(2,128)}), f32[2,8848]{1,0:T(2,128)}) %all-reduce.4.cloned.1.call-update) | async-done | bytes 70800 | tf_op jit(solution)/shard_map/psum | solution.py:465
  529.3 114.8 %reduce-scatter.5.cloned.1.call-done = bf16[384,256]{1,0:T(8,128)(2,1)} async-done(((bf16[12288,256]{1,0:T(8,128)(2,1)}), bf16[384,256]{1,0:T(8,128)(2,1)}) %reduce-scatter.5.cloned.1.call-update) | async-done | bytes 196624 | tf_op jit(solution)/shard_map/reduce_scatter | solution.py:443
  644.1 118.8 %reduce-scatter.3.cloned.1.call-done = bf16[384,256]{1,0:T(8,128)(2,1)} async-done(((bf16[12288,256]{1,0:T(8,128)(2,1)}), bf16[384,256]{1,0:T(8,128)(2,1)}) %reduce-scatter.3.cloned.1.call-update) | async-done | bytes 196624 | tf_op jit(solution)/shard_map/reduce_scatter | solution.py:447
  (208 shorter events, 59.5 us)
Async XLA Ops:
  8.0 6.4 copy-start.37
  8.0 6.3 copy-start.29
  8.0 6.3 copy-start.30
  8.0 6.3 copy-start.31
  8.1 6.3 copy-start.33
  8.1 6.3 copy-start.28
  8.1 7.7 copy-start.32
  8.1 12.6 %copy-start.11 = (bf16[1,98,16,512]{3,2,1,0:T(8,128)(2,1)S(1)}, bf16[1,98,16,512]{3,2,1,0:T(8,128)(2,1)}, u32[]{:S(2)}) copy-start(bf16[1,98,16,512]{3,2,1,0:T(8,128)(2,1)} %param.23) | copy-start | bytes 4816900
  8.1 41.1 %all-reduce.6.cloned.1.call-start = ((), (), s32[]{:S(2)}) async-start(), calls=%async_computation.7 | async-start | bytes 196608
  11.3 7.9 %collective-permute-start.2 = (bf16[384,256]{1,0:T(8,128)(2,1)S(1)}, bf16[384,256]{1,0:T(8,128)(2,1)S(1)}, u32[]{:S(2)}, u32[]{:S(2)}) collective-permute-start(bf16[384,256]{1,0:T(8,128)(2,1)S(1)} %constant_dynamic-slice_fusion.3), channel_id=1, source_target_pairs={{0,2},{2,0},{1,3},{3,1},{4,6},{6,4},{5,7},{7,5},{8,10},{10,8},{9,1... | collective-permute-start | bytes 589832 | tf_op jit(solution)/shard_map/ppermute | solution.py:365
  17.0 75.2 %all-gather.3.cloned.1.call-start = ((), (), s32[]{:S(2)}) async-start(), calls=%async_computation.2 | async-start | bytes 6488064 | tf_op jit(solution)/shard_map/all_gather | solution.py:385
  17.0 7.1 copy-start.20
  20.0 143.7 %all-gather.5.cloned.1.call-start = ((), (), s32[]{:S(2)}) async-start(), calls=%async_computation.3 | async-start | bytes 6488064 | tf_op jit(solution)/shard_map/all_gather | solution.py:386
  20.6 500.8 %all-reduce.4.cloned.1.call-start = ((), (), s32[]{:S(2)}) async-start(), calls=%async_computation.4 | async-start | bytes 143360 | tf_op jit(solution)/shard_map/psum | solution.py:465
  20.7 29.7 %copy-start.35 = (s32[64,64]{1,0:T(8,128)S(1)}, s32[64,64]{1,0:T(8,128)}, u32[]{:S(2)}) copy-start(s32[64,64]{1,0:T(8,128)} %constant.57.clone) | copy-start | bytes 49156
  21.8 36.7 %collective-permute-start = (bf16[98,8,512]{2,1,0:T(8,128)(2,1)}, bf16[98,8,512]{2,1,0:T(8,128)(2,1)S(1)}, u32[]{:S(2)}, u32[]{:S(2)}) collective-permute-start(bf16[98,8,512]{2,1,0:T(8,128)(2,1)} %get-tuple-element.89), channel_id=1, source_target_pairs={{0,2},{2,0},{1,3},{3,1},{4,6},{6,4},{5,7},{7,5},{8,10},{10,8},{9,1... | collective-permute-start | bytes 2408456 | tf_op jit(solution)/shard_map/ppermute | solution.py:365
  54.1 164.8 %copy-start.4 = (f32[1,4,64,256]{3,2,1,0:T(8,128)}, f32[1,4,64,256]{3,2,1,0:T(8,128)S(1)}, u32[]{:S(2)}) copy-start(f32[1,4,64,256]{3,2,1,0:T(8,128)S(1)} %reshape.403.bias_ref) | copy-start | bytes 786436
  54.1 164.7 %copy-start.6 = (f32[1,1,2,1024]{3,1,2,0:T(1,128)}, f32[1,1,2,1024]{3,1,2,0:T(1,128)S(1)}, u32[]{:S(2)}) copy-start(f32[1,1,2,1024]{3,1,2,0:T(1,128)S(1)} %copy.150) | copy-start | bytes 24580
  62.2 3.1 collective-permute-start.1
  63.0 2.3 collective-permute-start.3
  63.5 155.3 %copy-start.5 = (f32[8,512]{1,0:T(8,128)}, f32[8,512]{1,0:T(8,128)S(1)}, u32[]{:S(2)}) copy-start(f32[8,512]{1,0:T(8,128)S(1)} %concatenate.86.small_ref) | copy-start | bytes 49156
  65.3 2.7 copy-start.34
  168.6 4.0 copy-start.9
  180.3 38.5 %copy-start = (bf16[512,2048]{1,0:T(8,128)(2,1)}, bf16[512,2048]{1,0:T(8,128)(2,1)S(1)}, u32[]{:S(2)}) copy-start(bf16[512,2048]{1,0:T(8,128)(2,1)S(1)} %reshape.401.wfc1_ref) | copy-start | bytes 6291460
  193.1 1.6 copy-start.8
  193.8 25.0 %copy-start.3 = (bf16[64,8,2,256]{3,1,2,0:T(8,128)(2,1)}, bf16[64,8,2,256]{3,1,2,0:T(8,128)(2,1)S(1)}, u32[]{:S(2)}) copy-start(bf16[64,8,2,256]{3,1,2,0:T(8,128)(2,1)S(1)} %copy.151) | copy-start | bytes 1572868
  217.4 1.6 copy-start.1
  219.0 1.4 copy-start.2
  220.4 1.2 copy-start.7
  221.6 23.5 %copy-start.19 = (bf16[256,256,1]{1,0,2:T(8,128)(2,1)S(1)}, bf16[256,256,1]{1,0,2:T(8,128)(2,1)}, u32[]{:S(2)}) copy-start(bf16[256,256,1]{1,0,2:T(8,128)(2,1)} %constant.84) | copy-start | bytes 393220
  318.8 8.0 %copy-start.18 = (bf16[256,256,1]{1,0,2:T(8,128)(2,1)S(1)}, bf16[256,256,1]{1,0,2:T(8,128)(2,1)}, u32[]{:S(2)}) copy-start(bf16[256,256,1]{1,0,2:T(8,128)(2,1)} %constant.86) | copy-start | bytes 393220
  389.9 5.9 copy-start.36
  389.9 8.4 %copy-start.23 = (f32[8,512]{1,0:T(8,128)S(1)}, f32[8,512]{1,0:T(8,128)}, u32[]{:S(2)}) copy-start(f32[8,512]{1,0:T(8,128)} %get-tuple-element.29) | copy-start | bytes 49156
  389.9 8.4 %copy-start.27 = (f32[1,2048]{1,0:T(1,128)S(1)}, f32[1,2048]{1,0:T(1,128)}, u32[]{:S(2)}) copy-start(f32[1,2048]{1,0:T(1,128)} %get-tuple-element.30) | copy-start | bytes 24580
  389.9 8.4 %copy-start.17 = (f32[4,64,256]{2,1,0:T(8,128)S(1)}, f32[4,64,256]{2,1,0:T(8,128)}, u32[]{:S(2)}) copy-start(f32[4,64,256]{2,1,0:T(8,128)} %get-tuple-element.34) | copy-start | bytes 786436
  395.8 8.3 %copy-start.22 = (f32[8,512]{1,0:T(8,128)S(1)}, f32[8,512]{1,0:T(8,128)}, u32[]{:S(2)}) copy-start(f32[8,512]{1,0:T(8,128)} %get-tuple-element.32) | copy-start | bytes 49156
  395.8 8.3 %copy-start.26 = (f32[1,2048]{1,0:T(1,128)S(1)}, f32[1,2048]{1,0:T(1,128)}, u32[]{:S(2)}) copy-start(f32[1,2048]{1,0:T(1,128)} %get-tuple-element.33) | copy-start | bytes 24580
  404.8 239.3 %reduce-scatter.5.cloned.1.call-start = ((), (), s32[]{:S(2)}) async-start(), calls=%async_computation.6 | async-start | bytes 6488064 | tf_op jit(solution)/shard_map/reduce_scatter | solution.py:443
  419.1 1.4 copy-start.12
  419.2 343.8 %reduce-scatter.3.cloned.1.call-start = ((), (), s32[]{:S(2)}) async-start(), calls=%async_computation.5 | async-start | bytes 6488064 | tf_op jit(solution)/shard_map/reduce_scatter | solution.py:447
  452.8 2.9 copy-start.10
  455.4 69.0 %collective-permute-start.4 = (bf16[98,4,512]{2,0,1:T(8,128)(2,1)S(1)}, bf16[98,4,512]{2,0,1:T(8,128)(2,1)S(1)}, u32[]{:S(2)}, u32[]{:S(2)}) collective-permute-start(bf16[98,4,512]{2,0,1:T(8,128)(2,1)S(1)} %dynamic-slice_bitcast_fusion.2), channel_id=1, source_target_pairs={{0,1},{1,0},{2,3},{3,2},{4,5},{5,4},{6,7},{7,6},{8,9},{9,8},{10,11... | collective-permute-start | bytes 1204232 | tf_op jit(solution)/shard_map/ppermute | solution.py:365
  457.1 67.6 %collective-permute-start.5 = (bf16[98,4,512]{2,0,1:T(8,128)(2,1)S(1)}, bf16[98,4,512]{2,0,1:T(8,128)(2,1)S(1)}, u32[]{:S(2)}, u32[]{:S(2)}) collective-permute-start(bf16[98,4,512]{2,0,1:T(8,128)(2,1)S(1)} %dynamic-slice_bitcast_fusion.1), channel_id=1, source_target_pairs={{0,1},{1,0},{2,3},{3,2},{4,5},{5,4},{6,7},{7,6},{8,9},{9,8},{10,11... | collective-permute-start | bytes 1204232 | tf_op jit(solution)/shard_map/ppermute | solution.py:365
  524.9 2.0 copy-start.21
  525.1 240.4 %copy-start.25 = (f32[2,512]{1,0:T(2,128)S(1)}, f32[2,512]{1,0:T(2,128)}, u32[]{:S(2)}) copy-start(f32[2,512]{1,0:T(2,128)} %slice.269) | copy-start | bytes 12292
  525.1 241.0 %copy-start.24 = (f32[1024]{0:T(1024)S(1)}, f32[1024]{0:T(1024)}, u32[]{:S(2)}) copy-start(f32[1024]{0:T(1024)} %get-tuple-element.78) | copy-start | bytes 12292
  525.4 241.3 %collective-permute-start.6 = (bf16[98,8,512]{2,1,0:T(8,128)(2,1)S(1)}, bf16[98,8,512]{2,1,0:T(8,128)(2,1)S(1)}, u32[]{:S(2)}, u32[]{:S(2)}) collective-permute-start(bf16[98,8,512]{2,1,0:T(8,128)(2,1)S(1)} %copy.115), channel_id=1, source_target_pairs={{0,2},{2,0},{1,3},{3,1},{4,6},{6,4},{5,7},{7,5},{8,10},{10,8},{9,1... | collective-permute-start | bytes 2408456 | tf_op jit(solution)/shard_map/ppermute | solution.py:365
  764.0 5.7 collective-permute-start.7
  (4 other events, 3.6 us)
Sparse Core Ops, SparseCore 0:
  17.1 32.0 all-reduce.5
Sparse Core Ops, SparseCore 1:
  21.3 70.8 all-gather.2
  95.9 67.8 all-gather.4
  404.9 116.5 all-reduce.3
  528.1 116.0 reduce-scatter.4
  649.8 113.1 reduce-scatter.2

commit v2 on v1

--- a/solution.py
+++ b/solution.py
@@ -182,8 +182,41 @@
     return cdf
 
 
-def fwd_kernel(x_ref, small_ref, fc1b_ref, wqkv_ref, wproj_ref, wfc1_ref, wfc2_ref, bias_ref,
-               y_ref, qkv_s, o_s):
+CHUNK = 64
+COLS = 256
+BLOCKS = D // CHUNK
+
+
+def packed_places():
+    places = [(c, c, 0) for c in range(3)] + [(3, 3, 0)]
+    places += [(4 + n, 4, n * COLS) for n in range(FF // D)]
+    places += [(8 + n, 5, n * COLS) for n in range(FF // D)]
+    return places
+
+
+def unpack_weights(packed_ref, wqkv_s, wproj_s, wfc1_s, wfc2_s):
+    targets = [wqkv_s.at[0], wqkv_s.at[1], wqkv_s.at[2], wproj_s, wfc1_s, wfc2_s]
+    for piece, which, col in packed_places():
+        width = targets[which].shape[1] // 2
+        for half in range(2):
+            lanes = slice(half * width + col, half * width + col + COLS)
+            for block in range(BLOCKS):
+                targets[which][block * CHUNK : (block + 1) * CHUNK, lanes] = packed_ref[
+                    block, half, piece * CHUNK : (piece + 1) * CHUNK, :
+                ]
+
+
+def store_packed(packed_ref, piece, half, values):
+    for block in range(BLOCKS):
+        packed_ref[half, block, piece * CHUNK : (piece + 1) * CHUNK, :] = values[
+            block * CHUNK : (block + 1) * CHUNK
+        ]
+
+
+def fwd_kernel(x_ref, small_ref, fc1b_ref, packed_ref, bias_ref,
+               y_ref, qkv_s, o_s, wqkv_ref, wproj_ref, wfc1_ref, wfc2_ref):
+    unpack_weights(packed_ref, wqkv_ref, wproj_ref, wfc1_ref, wfc2_ref)
+
     def one_image(img, carry):
         x = x_ref[img].astype(F32)
         parts = forward_half(x, small_ref, wqkv_ref, wproj_ref, bias_ref, qkv_s, o_s, None)
@@ -200,9 +233,11 @@
     lax.fori_loop(0, x_ref.shape[0], one_image, 0)
 
 
-def bwd_kernel(x_ref, g_ref, small_ref, fc1b_ref, wqkv_ref, wproj_ref, wfc1_ref, wfc2_ref, bias_ref,
-               dx_ref, gqkv_ref, gproj_ref, gfc1_ref, gfc2_ref, gsmall_ref, gfc1b_ref, gtable_ref,
-               qkv_s, o_s, p_s, do_s, h_all, o_all, h2_all, dz_all, dy_all, a_all, du_all, dqkv_all):
+def bwd_kernel(x_ref, g_ref, small_ref, fc1b_ref, packed_ref, bias_ref,
+               dx_ref, gmats_ref, gsmall_ref, gfc1b_ref, gtable_ref,
+               qkv_s, o_s, p_s, do_s, h_all, o_all, h2_all, dz_all, dy_all, a_all, du_all, dqkv_all,
+               wqkv_ref, wproj_ref, wfc1_ref, wfc2_ref):
+    unpack_weights(packed_ref, wqkv_ref, wproj_ref, wfc1_ref, wfc2_ref)
     gsmall_ref[...] = jnp.zeros_like(gsmall_ref)
     gfc1b_ref[...] = jnp.zeros_like(gfc1b_ref)
     gtable_ref[...] = jnp.zeros_like(gtable_ref)
@@ -255,13 +290,17 @@
         return carry
 
     lax.fori_loop(0, x_ref.shape[0], one_image, 0)
-    for c in range(3):
-        gqkv_ref[c] = dot(h_all[...], dqkv_all[:, c * D : (c + 1) * D], 0, 0).astype(BF16)
-    gproj_ref[...] = dot(dy_all[...], o_all[...], 0, 0).astype(BF16)
-    for c in range(FF // 512):
-        cols = slice(c * 512, (c + 1) * 512)
-        gfc1_ref[:, cols] = dot(h2_all[...], du_all[:, cols], 0, 0).astype(BF16)
-        gfc2_ref[:, cols] = dot(dz_all[...], a_all[:, cols], 0, 0).astype(BF16)
+    for piece, which, col in packed_places():
+        for half in range(2):
+            if which < 3:
+                left, right = h_all[...], dqkv_all[:, pl.ds(which * D + half * COLS, COLS)]
+            elif which == 3:
+                left, right = dy_all[...], o_all[:, pl.ds(half * COLS, COLS)]
+            elif which == 4:
+                left, right = h2_all[...], du_all[:, pl.ds(half * (FF // 2) + col, COLS)]
+            else:
+                left, right = dz_all[...], a_all[:, pl.ds(half * (FF // 2) + col, COLS)]
+            store_packed(gmats_ref, piece, half, dot(left, right, 0, 0).astype(BF16))
 
 
 VMEM = pl.BlockSpec(memory_space=pltpu.VMEM)
@@ -281,12 +320,19 @@
     return pl.pallas_call(
         fwd_kernel,
         out_shape=jax.ShapeDtypeStruct(x.shape, BF16),
-        in_specs=[VMEM] * 8,
+        in_specs=[VMEM] * 5,
         out_specs=VMEM,
-        scratch_shapes=[pltpu.VMEM((IMG_ROWS, 3 * D), BF16), pltpu.VMEM((IMG_ROWS, D), BF16)],
+        scratch_shapes=[
+            pltpu.VMEM((IMG_ROWS, 3 * D), BF16),
+            pltpu.VMEM((IMG_ROWS, D), BF16),
+            pltpu.VMEM((3, D, D), BF16),
+            pltpu.VMEM((D, D), BF16),
+            pltpu.VMEM((D, FF), BF16),
+            pltpu.VMEM((D, FF), BF16),
+        ],
         compiler_params=pltpu.CompilerParams(vmem_limit_bytes=40 * 1024 * 1024),
         cost_estimate=layer_cost(images, 3),
-    )(x, small, fc1b, *mats, bias)
+    )(x, small, fc1b, mats, bias)
 
 
 def run_backward(x, grad, small, fc1b, mats, bias):
@@ -297,16 +343,13 @@
         bwd_kernel,
         out_shape=[
             shape(x.shape, BF16),
-            shape((3, D, D), BF16),
-            shape((D, D), BF16),
-            shape((D, FF), BF16),
-            shape((D, FF), BF16),
+            shape((2, BLOCKS, 12 * CHUNK, COLS), BF16),
             shape((8, D), F32),
             shape((1, FF), F32),
             shape((NG, WP, GH * WP), F32),
         ],
-        in_specs=[VMEM] * 9,
-        out_specs=[VMEM] * 8,
+        in_specs=[VMEM] * 6,
+        out_specs=[VMEM] * 5,
         scratch_shapes=[
             pltpu.VMEM((IMG_ROWS, 3 * D), BF16),
             pltpu.VMEM((IMG_ROWS, D), BF16),
@@ -320,10 +363,14 @@
             pltpu.VMEM((tokens, FF), BF16),
             pltpu.VMEM((tokens, FF), BF16),
             pltpu.VMEM((tokens, 3 * D), BF16),
+            pltpu.VMEM((3, D, D), BF16),
+            pltpu.VMEM((D, D), BF16),
+            pltpu.VMEM((D, FF), BF16),
+            pltpu.VMEM((D, FF), BF16),
         ],
         compiler_params=pltpu.CompilerParams(vmem_limit_bytes=56 * 1024 * 1024),
         cost_estimate=layer_cost(images, 9),
-    )(x, grad, small, fc1b, *mats, bias)
+    )(x, grad, small, fc1b, mats, bias)
 
 
 def pack_shard(qkv, proj, fc1, fc2):
@@ -344,21 +391,50 @@
     )
 
 
-def unpack_full(gathered, dp, tensor, rows, cols):
-    parts = gathered.reshape(dp, tensor, 12, rows, cols)
-    qkv = parts[:, :, 0:3].transpose(2, 0, 3, 1, 4).reshape(3, D, D)
-    proj = parts[:, :, 3].transpose(0, 2, 1, 3).reshape(D, D)
-    fc1 = parts[:, :, 4:8].transpose(0, 3, 1, 2, 4).reshape(D, FF)
-    fc2 = parts[:, :, 8:12].transpose(0, 3, 1, 2, 4).reshape(D, FF)
-    return qkv, proj, fc1, fc2
-
-
-def pack_full(qkv, proj, fc1, fc2, dp, tensor, rows, cols):
-    q = qkv.reshape(3, dp, rows, tensor, cols).transpose(1, 3, 0, 2, 4)
-    p = proj.reshape(1, dp, rows, tensor, cols).transpose(1, 3, 0, 2, 4)
-    f1 = fc1.reshape(dp, rows, tensor, FF // D, cols).transpose(0, 2, 3, 1, 4)
-    f2 = fc2.reshape(dp, rows, tensor, FF // D, cols).transpose(0, 2, 3, 1, 4)
-    return jnp.concatenate([q, p, f1, f2], axis=2).reshape(-1, cols)
+def to_blocks(gathered, dp, rows):
+    parts = gathered.reshape(BLOCKS, dp // BLOCKS, 2, 12, rows, COLS)
+    return parts.transpose(0, 2, 3, 1, 4, 5).reshape(BLOCKS, 2, 12 * CHUNK, COLS)
+
+
+def from_blocks(blocks, dp, rows):
+    parts = blocks.reshape(2, BLOCKS, 12, dp // BLOCKS, rows, COLS)
+    return parts.transpose(0, 1, 3, 2, 4, 5).reshape(2, dp, 12 * rows, COLS)
+
+
+def exchange_half(array, axis, name, bit):
+    bits = [(i, i ^ (1 << bit)) for i in range(lax.axis_size(name))]
+    which = (lax.axis_index(name) >> bit) & 1
+    there = lax.ppermute(half_of(array, 1 - which, axis), name, bits)
+    return (half_of(array, which, axis).astype(F32) + there.astype(F32)).astype(BF16)
+
+
+def total_of(array, dp):
+    array = array + swapped(array, "tensor")
+    array = array + swapped(array, "pipe")
+    for bit in range(dp.bit_length() - 1):
+        array = array + lax.ppermute(array, "dp", [(i, i ^ (1 << bit)) for i in range(dp)])
+    return array
+
+
+def scatter_sum(blocks, dp, rows):
+    array = from_blocks(blocks, dp, rows)
+    array = exchange_half(array, 0, "tensor", 0)
+    levels = dp.bit_length() - 1
+    array = array.reshape((2,) * levels + (2, 6 * rows, COLS))
+    last = levels - 1
+    done = []
+    for part in range(2):
+        one = array[..., part * (COLS // 2) : (part + 1) * (COLS // 2)]
+        if part == 0:
+            one = exchange_half(one, levels, "pipe", 0)
+            one = exchange_half(one, last, "dp", 0)
+        else:
+            one = exchange_half(one, last, "dp", 0)
+            one = exchange_half(one, levels, "pipe", 0)
+        for level in range(levels - 1):
+            one = exchange_half(one, level, "dp", levels - 1 - level)
+        done.append(one.reshape(6 * rows, COLS // 2))
+    return jnp.concatenate(done, axis=1)
 
 
 def swapped(array, axis):
@@ -375,7 +451,7 @@
     pipe = lax.axis_index("pipe")
     tensor = lax.axis_index("tensor")
     first = pipe == 0
-    dp_n, tensor_n = lax.axis_size("dp"), lax.axis_size("tensor")
+    dp_n = lax.axis_size("dp")
     rows, cols = w_proj.shape[1], w_proj.shape[2]
 
     shard = pack_shard(w_qkv[0], w_proj[0], w_fc1[0], w_fc2[0])
@@ -385,7 +461,7 @@
         lax.all_gather(jnp.where(first, kept, got), ALL_AXES, axis=0, tiled=True),
         lax.all_gather(jnp.where(first, got, kept), ALL_AXES, axis=0, tiled=True),
     ]
-    mats = [unpack_full(g, dp_n, tensor_n, rows, cols) for g in gathered]
+    mats = [to_blocks(gathered[0], dp_n, rows)]
 
     heads_here = rel_table.shape[1]
     sizes = (2 * D, 2 * D, 2 * D, 2 * cols, fc1_bias.shape[1], heads_here * TABLE)
@@ -437,16 +513,18 @@
     c_in = placed(order[1], c_tokens, "rs,sbd->brd")
 
     y0 = run_forward(x_in, smalls[0], hidden[0], mats[0], biases[0])
+    y0, second_mats = lax.optimization_barrier((y0, gathered[1]))
     y0 = placed(order[1] @ order[0].T, y0, "rs,bsd->brd")
-    back1 = run_backward(y0, c_in, smalls[1], hidden[1], mats[1], biases[1])
+    back1 = run_backward(y0, c_in, smalls[1], hidden[1], to_blocks(second_mats, dp_n, rows), biases[1])
     g_mid = placed(order[0] @ order[1].T, back1[0], "rs,bsd->brd")
     g1 = lax.psum_scatter(
-        pack_full(*back1[1:5], dp_n, tensor_n, rows, cols), ALL_AXES, scatter_dimension=0, tiled=True
+        from_blocks(back1[1], dp_n, rows).reshape(-1, cols),
+        ("tensor", "dp", "pipe"),
+        scatter_dimension=0,
+        tiled=True,
     )
     back0 = run_backward(x_in, g_mid, smalls[0], hidden[0], mats[0], biases[0])
-    g0 = lax.psum_scatter(
-        pack_full(*back0[1:5], dp_n, tensor_n, rows, cols), ALL_AXES, scatter_dimension=0, tiled=True
-    )
+    g0 = scatter_sum(back0[1], dp_n, rows)
 
     other = swapped(jnp.where(first, g1, g0), "pipe")
     mine = jnp.where(first, g0, g1)
@@ -458,11 +536,11 @@
     hot = rel_one_hot().reshape(TABLE, WP * WP)
 
     def small_grads(back):
-        scores = back[7].reshape(NG, WP, GH, WP).transpose(0, 2, 1, 3).reshape(HEADS, WP * WP)
+        scores = back[4].reshape(NG, WP, GH, WP).transpose(0, 2, 1, 3).reshape(HEADS, WP * WP)
         table = lax.dot_general(scores, hot, (((1,), (1,)), ((), ())), precision=HIGHEST)
-        return jnp.concatenate([back[5].reshape(-1), back[6].reshape(-1), table.reshape(-1)])
-
-    summed = lax.psum(jnp.stack([small_grads(back0), small_grads(back1)]), ALL_AXES)
+        return jnp.concatenate([back[2].reshape(-1), back[3].reshape(-1), table.reshape(-1)])
+
+    summed = total_of(jnp.stack([small_grads(back0), small_grads(back1)]), dp_n)
     summed = jnp.where(first, summed[0], summed[1])
     rows_g = summed[: 8 * D].reshape(8, D)
     gains_g = jnp.stack([rows_g[0], rows_g[2]])

time: 792 us -> 458 us (0.58)
  waiting for transfers between devices: 412 us -> 197 us
  local copies, waits for them, and re-layouts: 150 us -> 31.9 us
  starting transfers between devices: 9.2 us -> 20.7 us
  other arithmetic: 26.5 us -> 17.6 us
    reduce_scatter x2 -> x1, waiting for transfers between devices: 234 us -> 40.4 us  [on_device(): lax.psum_scatter(from_blocks(back1[1], dp_n, rows).reshape(-1, cols), ('t...]
    reshape x22 -> x6, local copies, waits for them, and re-layouts: 72.3 us -> 1.94 us  [small_grads(): back[4].reshape(NG, WP, GH, WP).transpose(0, 2, 1, 3)]
    psum x1 -> x0, waiting for transfers between devices: 64 us -> none  [on_device(): lax.psum(jnp.stack([small_grads(back0), small_grads(back1)]), ALL_AXES)]
    ppermute x0 -> x12, waiting for transfers between devices: none -> 59 us  [the longest x9 51.5 us: exchange_half(): there = lax.ppermute(half_of(array, 1 - which, axis), name, bits)]
    all_gather x1, waiting for transfers between devices: 63.8 us -> 44.7 us  [on_device(): lax.all_gather(jnp.where(first, got, kept), ALL_AXES, axis=0, tiled=True)]
    slice x6 -> x1, local copies, waits for them, and re-layouts: 16.5 us -> 0.86 us  [scatter_sum(): one = array[..., part * (COLS // 2):(part + 1) * (COLS // 2)]]
    concatenate x4 -> x2, other arithmetic: 15.5 us -> 0.01 us  [small_grads(): jnp.concatenate([back[2].reshape(-1), back[3].reshape(-1), table.reshape(...]
    unnamed x106 -> x86, local copies, waits for them, and re-layouts: 21.5 us -> 7.8 us
  transfers between devices with their start and end apart: 14 -> 26, of which waited for: 8 -> 17; matrix products, arithmetic and copies ran while one was open for 12% -> 10% of each run, Pallas kernels for 0% -> 5%
where the time goes in v2:
time: 458 us; the launch traced here: 450 us
  waiting for transfers between devices  197 us (43%)
  Pallas kernels  149 us (33%)
  local copies, waits for them, and re-layouts  31.9 us (7%)
  starting transfers between devices  20.7 us (5%)
  between operations  18.2 us (4%)
  other arithmetic  17.6 us (4%)
  matrix products  16.2 us (4%)
    pallas_call x2, Pallas kernels, run_backward(): pl.pallas_call(bwd_kernel, out_shape=[shape(x.shape, BF16), shape((2, BLO...  125 us
    ppermute x9, waiting for transfers between devices, exchange_half(): there = lax.ppermute(half_of(array, 1 - which, axis), name, bits)  51.5 us
    all_gather x1, waiting for transfers between devices, on_device(): lax.all_gather(jnp.where(first, got, kept), ALL_AXES, axis=0, tiled=True)  44.7 us
    reduce_scatter x1, waiting for transfers between devices, on_device(): lax.psum_scatter(from_blocks(back1[1], dp_n, rows).reshape(-1, cols), ('t...  40.4 us
    unnamed x5, waiting for transfers between devices  25.1 us
    pallas_call x1, Pallas kernels, run_forward(): pl.pallas_call(fwd_kernel, out_shape=jax.ShapeDtypeStruct(x.shape, BF16),...  24.2 us
    all_gather x1, waiting for transfers between devices, on_device(): lax.all_gather(jnp.where(first, kept, got), ALL_AXES, axis=0, tiled=True)  24.2 us
    dynamic_slice x16, local copies, waits for them, and re-layouts, half_of(): return lax.dynamic_slice_in_dim(array, which * size, size, axis)  9.95 us
  transfers between devices with their start and end apart: 26, of which 17 were waited for; matrix products, arithmetic and copies ran while one was open for 10% of the time, Pallas kernels for 5%

profile of v2, /device:TPU:0, one launch (start us, length us, event | category | flops | bytes accessed | tf_op | source)
XLA Modules:
  0.0 450.2 jit_solution(4378713600933318739)
XLA Ops:
  9.2 1.1 reshape_squeeze.38
  11.3 3.0 collective-permute-start.2
  17.0 2.2 collective-permute-done.2
  20.7 1.1 constant_dynamic-slice_fusion.15
  21.8 1.7 collective-permute-start
  24.6 24.6 %all-reduce.3.cloned.1.call-done = f32[23840]{0:T(1024)} async-done(((f32[23840]{0:T(1024)}), f32[23840]{0:T(1024)}) %all-reduce.3.cloned.1.call-update) | async-done | bytes 95376
  50.4 3.3 fusion.18
  54.2 3.3 fusion.24
  58.5 2.0 bitcast_select_fusion
  63.3 1.1 broadcast_add_fusion.bias_ref
  64.4 1.2 broadcast_select_fusion.2
  66.4 1.5 fusion.12.g_ref
  68.0 24.2 %all-gather.3.cloned.1.call-done = bf16[12288,256]{1,0:T(8,128)(2,1)} async-done(((bf16[384,256]{1,0:T(8,128)(2,1)}), bf16[12288,256]{1,0:T(8,128)(2,1)}) %all-gather.3.cloned.1.call-update) | async-done | bytes 6291472 | tf_op jit(solution)/shard_map/all_gather | solution.py:461
  92.2 2.8 copy-done.3
  95.0 24.2 %shard_map.302 = bf16[4,256,512]{2,1,0:T(8,128)(2,1)S(1)} custom-call(bf16[4,256,512]{2,1,0:T(8,128)(2,1)S(1)} %fusion.11.x_ref, f32[8,512]{1,0:T(8,128)S(1)} %concatenate.83.small_ref, f32[1,2048]{1,0:T(1,128)S(1)} %bitcast.170, bf16[8,2,768,256]{3,2,1,0:T(8,128)(2,1)S(1)} %bitcast.173, f32[1,4,64,256]{3,2,1,0:T(8,128)S(1)} %reshape.347.bias_ref), custom_call_target="tpu_custom_call" | custom-call | flops 19327352832 | bytes 20000000 | tf_op jit(solution)/shard_map/pallas_call | solution.py:320
  119.2 44.7 %all-gather.5.cloned.1.call-done = bf16[12288,256]{1,0:T(8,128)(2,1)} async-done(((bf16[384,256]{1,0:T(8,128)(2,1)}), bf16[12288,256]{1,0:T(8,128)(2,1)}) %all-gather.5.cloned.1.call-update) | async-done | bytes 6291472 | tf_op jit(solution)/shard_map/all_gather | solution.py:462
  163.9 1.4 fusion.13.x_ref
  165.3 62.5 %shard_map.303 = (bf16[4,256,512]{2,1,0:T(8,128)(2,1)}, bf16[2,8,768,256]{3,2,1,0:T(8,128)(2,1)}, f32[8,512]{1,0:T(8,128)}, f32[1,2048]{1,0:T(1,128)}, f32[4,64,256]{2,1,0:T(8,128)}) custom-call(bf16[4,256,512]{2,1,0:T(8,128)(2,1)} %fusion.13.x_ref, bf16[4,256,512]{2,1,0:T(8,128)(2,1)} %fusion.12.g_ref, f32[8,512]{1,0:T(8,128)} %concatenate.86.small_ref, ...), custom_call_target="tpu_custom_call" | custom-call | flops 57982058496 | bytes 20000000 | tf_op jit(solution)/shard_map/pallas_call | solution.py:342
  227.8 2.6 fusion.14.g_ref
  230.5 62.0 %shard_map.304 = (bf16[4,256,512]{2,1,0:T(8,128)(2,1)}, bf16[2,8,768,256]{3,2,1,0:T(8,128)(2,1)}, f32[8,512]{1,0:T(8,128)}, f32[1,2048]{1,0:T(1,128)}, f32[4,64,256]{2,1,0:T(8,128)}) custom-call(bf16[4,256,512]{2,1,0:T(8,128)(2,1)} %copy-done.4, bf16[4,256,512]{2,1,0:T(8,128)(2,1)} %fusion.14.g_ref, f32[8,512]{1,0:T(8,128)} %copy-done.1, ...), custom_call_target="tpu_custom_call" | custom-call | flops 57982058496 | bytes 20000000 | tf_op jit(solution)/shard_map/pallas_call | solution.py:342
  292.5 1.2 reshape.350
  294.0 1.4 fusion.6
  296.1 1.4 fusion.5
  299.2 1.5 collective-permute-start.8
  300.8 3.8 constant_dynamic-slice_fusion.11
  306.2 3.2 collective-permute-done.9
  309.5 1.6 collective-permute-start.10
  312.2 1.7 collective-permute-done.10
  313.9 1.9 collective-permute-start.11
  316.7 2.6 collective-permute-done.11
  320.7 3.8 add_convert_fusion
  328.2 1.5 collective-permute-start.17
  329.7 1.4 bitcast_select_fusion.5
  331.1 1.2 bitcast_select_fusion.3
  332.3 11.8 %collective-permute-done.13 = bf16[2,2,2,1,384,128]{5,4,3,2,1,0:T(8,128)(2,1)} collective-permute-done((bf16[2,2,2,1,384,128]{5,4,3,2,1,0:T(8,128)(2,1)}, bf16[2,2,2,1,384,128]{5,4,3,2,1,0:T(8,128)(2,1)}, u32[]{:S(2)}, u32[]{:S(2)}) %collective-permute-start.13) | collective-permute-done | bytes 786464 | tf_op jit(solution)/shard_map/ppermute | solution.py:407
  344.1 1.4 add_convert_fusion.2
  346.4 1.8 collective-permute-start.18
  348.9 4.9 %collective-permute-done.14 = bf16[2,2,1,1,384,128]{5,4,3,2,1,0:T(8,128)(2,1)S(1)} collective-permute-done((bf16[2,2,1,1,384,128]{5,4,3,2,1,0:T(8,128)(2,1)S(1)}, bf16[2,2,1,1,384,128]{5,4,3,2,1,0:T(8,128)(2,1)S(1)}, u32[]{:S(2)}, u32[]{:S(2)}) %collective-permute-start.14) | collective-permute-done | bytes 393248 | tf_op jit(solution)/shard_map/ppermute | solution.py:407
  353.9 1.4 collective-permute-start.15
  355.3 6.8 %collective-permute-done.18 = bf16[2,2,1,1,384,128]{5,4,3,2,1,0:T(8,128)(2,1)S(1)} collective-permute-done((bf16[2,2,1,1,384,128]{5,4,3,2,1,0:T(8,128)(2,1)S(1)}, bf16[2,2,1,1,384,128]{5,4,3,2,1,0:T(8,128)(2,1)S(1)}, u32[]{:S(2)}, u32[]{:S(2)}) %collective-permute-start.18) | collective-permute-done | bytes 393248 | tf_op jit(solution)/shard_map/ppermute | solution.py:407
  362.3 1.1 collective-permute-start.19
  363.3 12.1 %collective-permute-done.15 = bf16[1,2,1,1,384,128]{5,4,3,2,1,0:T(8,128)(2,1)S(1)} collective-permute-done((bf16[1,2,1,1,384,128]{5,4,3,2,1,0:T(8,128)(2,1)S(1)}, bf16[1,2,1,1,384,128]{5,4,3,2,1,0:T(8,128)(2,1)S(1)}, u32[]{:S(2)}, u32[]{:S(2)}) %collective-permute-start.15) | collective-permute-done | bytes 196640 | tf_op jit(solution)/shard_map/ppermute | solution.py:407
  375.6 5.0 %collective-permute-done.19 = bf16[1,2,1,1,384,128]{5,4,3,2,1,0:T(8,128)(2,1)S(1)} collective-permute-done((bf16[1,2,1,1,384,128]{5,4,3,2,1,0:T(8,128)(2,1)S(1)}, bf16[1,2,1,1,384,128]{5,4,3,2,1,0:T(8,128)(2,1)S(1)}, u32[]{:S(2)}, u32[]{:S(2)}) %collective-permute-start.19) | collective-permute-done | bytes 196640 | tf_op jit(solution)/shard_map/ppermute | solution.py:407
  380.7 7.1 %collective-permute-done.16 = bf16[1,1,1,1,384,128]{5,4,3,2,1,0:T(8,128)(2,1)S(1)} collective-permute-done((bf16[1,1,1,1,384,128]{5,4,3,2,1,0:T(8,128)(2,1)S(1)}, bf16[1,1,1,1,384,128]{5,4,3,2,1,0:T(8,128)(2,1)S(1)}, u32[]{:S(2)}, u32[]{:S(2)}) %collective-permute-start.16) | collective-permute-done | bytes 98336 | tf_op jit(solution)/shard_map/ppermute | solution.py:407
  387.8 3.9 collective-permute-done.20
  391.8 40.4 %reduce-scatter.2.cloned.1.call-done = bf16[384,256]{1,0:T(8,128)(2,1)} async-done(((bf16[12288,256]{1,0:T(8,128)(2,1)}), bf16[384,256]{1,0:T(8,128)(2,1)}) %reduce-scatter.2.cloned.1.call-update) | async-done | bytes 196624 | tf_op jit(solution)/shard_map/reduce_scatter | solution.py:520
  433.2 1.7 collective-permute-start.21
  436.6 1.7 copy.85
  (206 shorter events, 32.4 us)
Async XLA Ops:
  8.0 6.5 %copy-start.30 = (u32[32]{0:T(128)S(1)}, u32[32]{0:T(128)}, u32[]{:S(2)}) copy-start(u32[32]{0:T(128)} %constant.91) | copy-start | bytes 388
  8.0 6.3 %copy-start.22 = (f32[1,2,512]{2,1,0:T(2,128)S(1)}, f32[1,2,512]{2,1,0:T(2,128)}, u32[]{:S(2)}) copy-start(f32[1,2,512]{2,1,0:T(2,128)} %param.25) | copy-start | bytes 12292
  8.0 6.3 %copy-start.23 = (f32[1,2,512]{2,1,0:T(2,128)S(1)}, f32[1,2,512]{2,1,0:T(2,128)}, u32[]{:S(2)}) copy-start(f32[1,2,512]{2,1,0:T(2,128)} %param.26) | copy-start | bytes 12292
  8.0 6.3 %copy-start.24 = (f32[1,2,512]{2,1,0:T(2,128)S(1)}, f32[1,2,512]{2,1,0:T(2,128)}, u32[]{:S(2)}) copy-start(f32[1,2,512]{2,1,0:T(2,128)} %param.31) | copy-start | bytes 12292
  8.1 6.3 %copy-start.26 = (f32[1,2,256]{2,1,0:T(2,128)S(1)}, f32[1,2,256]{2,1,0:T(2,128)}, u32[]{:S(2)}) copy-start(f32[1,2,256]{2,1,0:T(2,128)} %param.28) | copy-start | bytes 6148
  8.1 6.3 %copy-start.21 = (f32[1,8,169]{2,1,0:T(8,128)S(1)}, f32[1,8,169]{2,1,0:T(8,128)}, u32[]{:S(2)}) copy-start(f32[1,8,169]{2,1,0:T(8,128)} %param.29) | copy-start | bytes 16228
  8.1 7.7 %copy-start.25 = (f32[1,1024]{1,0:T(1,128)S(1)}, f32[1,1024]{1,0:T(1,128)}, u32[]{:S(2)}) copy-start(f32[1,1024]{1,0:T(1,128)} %param.33) | copy-start | bytes 12292
  8.1 41.1 %all-reduce.3.cloned.1.call-start = ((), (), s32[]{:S(2)}) async-start(), calls=%async_computation.4 | async-start | bytes 196608
  9.1 11.5 %copy-start.9 = (bf16[1,98,16,512]{3,2,1,0:T(8,128)(2,1)S(1)}, bf16[1,98,16,512]{3,2,1,0:T(8,128)(2,1)}, u32[]{:S(2)}) copy-start(bf16[1,98,16,512]{3,2,1,0:T(8,128)(2,1)} %param.23) | copy-start | bytes 4816900
  11.3 7.9 %collective-permute-start.2 = (bf16[384,256]{1,0:T(8,128)(2,1)S(1)}, bf16[384,256]{1,0:T(8,128)(2,1)S(1)}, u32[]{:S(2)}, u32[]{:S(2)}) collective-permute-start(bf16[384,256]{1,0:T(8,128)(2,1)S(1)} %constant_dynamic-slice_fusion.13), channel_id=1, source_target_pairs={{0,2},{2,0},{1,3},{3,1},{4,6},{6,4},{5,7},{7,5},{8,10},{10,8},{9,1... | collective-permute-start | bytes 589832 | tf_op jit(solution)/shard_map/ppermute | solution.py:441
  17.0 75.2 %all-gather.3.cloned.1.call-start = ((), (), s32[]{:S(2)}) async-start(), calls=%async_computation.1 | async-start | bytes 6488064 | tf_op jit(solution)/shard_map/all_gather | solution.py:461
  20.0 143.9 %all-gather.5.cloned.1.call-start = ((), (), s32[]{:S(2)}) async-start(), calls=%async_computation.2 | async-start | bytes 6488064 | tf_op jit(solution)/shard_map/all_gather | solution.py:462
  20.6 3.5 copy-start.16
  20.6 411.5 %reduce-scatter.2.cloned.1.call-start = ((), (), s32[]{:S(2)}) async-start(), calls=%async_computation.3 | async-start | bytes 6488064 | tf_op jit(solution)/shard_map/reduce_scatter | solution.py:520
  21.8 28.6 %copy-start.28 = (s32[64,64]{1,0:T(8,128)S(1)}, s32[64,64]{1,0:T(8,128)}, u32[]{:S(2)}) copy-start(s32[64,64]{1,0:T(8,128)} %constant.69.clone) | copy-start | bytes 49156
  21.8 36.7 %collective-permute-start = (bf16[98,8,512]{2,1,0:T(8,128)(2,1)}, bf16[98,8,512]{2,1,0:T(8,128)(2,1)}, u32[]{:S(2)}, u32[]{:S(2)}) collective-permute-start(bf16[98,8,512]{2,1,0:T(8,128)(2,1)} %get-tuple-element.79), channel_id=1, source_target_pairs={{0,2},{2,0},{1,3},{3,1},{4,6},{6,4},{5,7},{7,5},{8,10},{10,8},{9,1... | collective-permute-start | bytes 2408456 | tf_op jit(solution)/shard_map/ppermute | solution.py:441
  54.1 38.1 %copy-start = (f32[1,4,64,256]{3,2,1,0:T(8,128)}, f32[1,4,64,256]{3,2,1,0:T(8,128)S(1)}, u32[]{:S(2)}) copy-start(f32[1,4,64,256]{3,2,1,0:T(8,128)S(1)} %reshape.347.bias_ref) | copy-start | bytes 786436
  54.1 38.1 %copy-start.2 = (f32[1,1,2,1024]{3,1,2,0:T(1,128)}, f32[1,1,2,1024]{3,1,2,0:T(1,128)S(1)}, u32[]{:S(2)}) copy-start(f32[1,1,2,1024]{3,1,2,0:T(1,128)S(1)} %copy.100) | copy-start | bytes 24580
  61.3 3.1 collective-permute-start.1
  62.1 2.3 collective-permute-start.3
  62.6 29.5 %copy-start.1 = (f32[8,512]{1,0:T(8,128)}, f32[8,512]{1,0:T(8,128)S(1)}, u32[]{:S(2)}) copy-start(f32[8,512]{1,0:T(8,128)S(1)} %concatenate.83.small_ref) | copy-start | bytes 49156
  66.1 53.2 %copy-start.4 = (bf16[4,256,512]{2,1,0:T(8,128)(2,1)}, bf16[4,256,512]{2,1,0:T(8,128)(2,1)S(1)}, u32[]{:S(2)}) copy-start(bf16[4,256,512]{2,1,0:T(8,128)(2,1)S(1)} %fusion.11.x_ref) | copy-start | bytes 3145732
  94.9 68.9 %copy-start.15 = (bf16[256,256,1]{1,0,2:T(8,128)(2,1)S(1)}, bf16[256,256,1]{1,0,2:T(8,128)(2,1)}, u32[]{:S(2)}) copy-start(bf16[256,256,1]{1,0,2:T(8,128)(2,1)} %constant.96) | copy-start | bytes 393220
  165.3 62.5 %copy-start.14 = (bf16[256,256,1]{1,0,2:T(8,128)(2,1)S(1)}, bf16[256,256,1]{1,0,2:T(8,128)(2,1)}, u32[]{:S(2)}) copy-start(bf16[256,256,1]{1,0,2:T(8,128)(2,1)} %constant.98) | copy-start | bytes 393220
  292.5 3.0 copy-start.18
  292.5 3.1 copy-start.20
  292.5 3.1 copy-start.13
  297.8 1.3 collective-permute-start.7
  298.6 17.2 %copy-start.6 = (bf16[4,512,196]{1,2,0:T(8,128)(2,1)}, bf16[4,512,196]{1,2,0:T(8,128)(2,1)S(1)}, u32[]{:S(2)}) copy-start(bf16[4,512,196]{1,2,0:T(8,128)(2,1)S(1)} %convolution_convert_fusion.4) | copy-start | bytes 2408452
  299.2 5.4 %collective-permute-start.8 = (f32[2,8848]{1,0:T(2,128)S(1)}, f32[2,8848]{1,0:T(2,128)S(1)}, u32[]{:S(2)}, u32[]{:S(2)}) collective-permute-start(f32[2,8848]{1,0:T(2,128)S(1)} %fusion.42), channel_id=1, source_target_pairs={{0,2},{2,0},{1,3},{3,1},{4,6},{6,4},{5,7},{7,5},{8,10},{10,8},{9,1... | collective-permute-start | bytes 212360 | tf_op jit(solution)/shard_map/ppermute | solution.py:441
  304.6 16.1 %collective-permute-start.12 = (bf16[1,8,768,256]{3,2,1,0:T(8,128)(2,1)}, bf16[1,8,768,256]{3,2,1,0:T(8,128)(2,1)}, u32[]{:S(2)}, u32[]{:S(2)}) collective-permute-start(bf16[1,8,768,256]{3,2,1,0:T(8,128)(2,1)} %constant_dynamic-slice_fusion.11), channel_id=1, source_target_pairs={{0,1},{1,0},{2,3},{3,2},{4,5},{5,4},{6,7},{7,6},{8,9},{9,8},{10,11... | collective-permute-start | bytes 9437192 | tf_op jit(solution)/shard_map/ppermute | solution.py:407
  304.8 4.7 %collective-permute-start.9 = (f32[2,8848]{1,0:T(2,128)S(1)}, f32[2,8848]{1,0:T(2,128)S(1)}, u32[]{:S(2)}, u32[]{:S(2)}) collective-permute-start(f32[2,8848]{1,0:T(2,128)S(1)} %fusion.60), channel_id=1, source_target_pairs={{0,4},{4,0},{8,12},{12,8},{16,20},{20,16},{24,28},{28,24},{1,5},{5... | collective-permute-start | bytes 212360 | tf_op jit(solution)/shard_map/ppermute | solution.py:415
  306.2 10.4 %copy-start.8 = (bf16[4,512,196]{1,2,0:T(8,128)(2,1)}, bf16[4,512,196]{1,2,0:T(8,128)(2,1)S(1)}, u32[]{:S(2)}) copy-start(bf16[4,512,196]{1,2,0:T(8,128)(2,1)S(1)} %convolution_convert_fusion.5) | copy-start | bytes 2408452
  309.5 4.4 collective-permute-start.10
  311.9 17.7 %collective-permute-start.4 = (bf16[98,4,512]{2,0,1:T(8,128)(2,1)}, bf16[98,4,512]{2,0,1:T(8,128)(2,1)}, u32[]{:S(2)}, u32[]{:S(2)}) collective-permute-start(bf16[98,4,512]{2,0,1:T(8,128)(2,1)} %dynamic-slice_bitcast_fusion.2), channel_id=1, source_target_pairs={{0,1},{1,0},{2,3},{3,2},{4,5},{5,4},{6,7},{7,6},{8,9},{9,8},{10,11... | collective-permute-start | bytes 1204232 | tf_op jit(solution)/shard_map/ppermute | solution.py:441
  313.9 5.3 %collective-permute-start.11 = (f32[2,8848]{1,0:T(2,128)S(1)}, f32[2,8848]{1,0:T(2,128)S(1)}, u32[]{:S(2)}, u32[]{:S(2)}) collective-permute-start(f32[2,8848]{1,0:T(2,128)S(1)} %add.221), channel_id=1, source_target_pairs={{0,16},{4,20},{8,24},{12,28},{16,0},{20,4},{24,8},{28,12},{1,17},{... | collective-permute-start | bytes 212360 | tf_op jit(solution)/shard_map/ppermute | solution.py:415
  316.7 14.4 %collective-permute-start.5 = (bf16[98,4,512]{2,0,1:T(8,128)(2,1)}, bf16[98,4,512]{2,0,1:T(8,128)(2,1)}, u32[]{:S(2)}, u32[]{:S(2)}) collective-permute-start(bf16[98,4,512]{2,0,1:T(8,128)(2,1)} %dynamic-slice_bitcast_fusion.1), channel_id=1, source_target_pairs={{0,1},{1,0},{2,3},{3,2},{4,5},{5,4},{6,7},{7,6},{8,9},{9,8},{10,11... | collective-permute-start | bytes 1204232 | tf_op jit(solution)/shard_map/ppermute | solution.py:441
  326.4 17.7 %collective-permute-start.13 = (bf16[2,2,2,1,384,128]{5,4,3,2,1,0:T(8,128)(2,1)}, bf16[2,2,2,1,384,128]{5,4,3,2,1,0:T(8,128)(2,1)}, u32[]{:S(2)}, u32[]{:S(2)}) collective-permute-start(bf16[2,2,2,1,384,128]{5,4,3,2,1,0:T(8,128)(2,1)} %constant_dynamic-slice_fusion.10), channel_id=1, source_target_pairs={{0,2},{2,0},{1,3},{3,1},{4,6},{6,4},{5,7},{7,5},{8,10},{10,8},{9,1... | collective-permute-start | bytes 2359304 | tf_op jit(solution)/shard_map/ppermute | solution.py:407
  328.1 3.0 copy-start.7
  328.2 17.9 %collective-permute-start.17 = (bf16[2,2,1,2,384,128]{5,4,3,2,1,0:T(8,128)(2,1)S(1)}, bf16[2,2,1,2,384,128]{5,4,3,2,1,0:T(8,128)(2,1)S(1)}, u32[]{:S(2)}, u32[]{:S(2)}) collective-permute-start(bf16[2,2,1,2,384,128]{5,4,3,2,1,0:T(8,128)(2,1)S(1)} %constant_dynamic-slice_fusion.6), channel_id=1, source_target_pairs={{0,4},{4,0},{8,12},{12,8},{16,20},{20,16},{24,28},{28,24},{1,5},{5... | collective-permute-start | bytes 2359304 | tf_op jit(solution)/shard_map/ppermute | solution.py:407
  345.5 8.3 %collective-permute-start.14 = (bf16[2,2,1,1,384,128]{5,4,3,2,1,0:T(8,128)(2,1)S(1)}, bf16[2,2,1,1,384,128]{5,4,3,2,1,0:T(8,128)(2,1)S(1)}, u32[]{:S(2)}, u32[]{:S(2)}) collective-permute-start(bf16[2,2,1,1,384,128]{5,4,3,2,1,0:T(8,128)(2,1)S(1)} %constant_dynamic-slice_fusion.9), channel_id=1, source_target_pairs={{0,4},{4,0},{8,12},{12,8},{16,20},{20,16},{24,28},{28,24},{1,5},{5... | collective-permute-start | bytes 1179656 | tf_op jit(solution)/shard_map/ppermute | solution.py:407
  346.4 15.7 %collective-permute-start.18 = (bf16[2,2,1,1,384,128]{5,4,3,2,1,0:T(8,128)(2,1)S(1)}, bf16[2,2,1,1,384,128]{5,4,3,2,1,0:T(8,128)(2,1)S(1)}, u32[]{:S(2)}, u32[]{:S(2)}) collective-permute-start(bf16[2,2,1,1,384,128]{5,4,3,2,1,0:T(8,128)(2,1)S(1)} %constant_dynamic-slice_fusion.5), channel_id=1, source_target_pairs={{0,2},{2,0},{1,3},{3,1},{4,6},{6,4},{5,7},{7,5},{8,10},{10,8},{9,1... | collective-permute-start | bytes 1179656 | tf_op jit(solution)/shard_map/ppermute | solution.py:407
  348.6 87.4 %collective-permute-start.6 = (bf16[98,8,512]{2,1,0:T(8,128)(2,1)S(1)}, bf16[98,8,512]{2,1,0:T(8,128)(2,1)S(1)}, u32[]{:S(2)}, u32[]{:S(2)}) collective-permute-start(bf16[98,8,512]{2,1,0:T(8,128)(2,1)S(1)} %copy.79), channel_id=1, source_target_pairs={{0,2},{2,0},{1,3},{3,1},{4,6},{6,4},{5,7},{7,5},{8,10},{10,8},{9,1... | collective-permute-start | bytes 2408456 | tf_op jit(solution)/shard_map/ppermute | solution.py:441
  353.9 21.5 %collective-permute-start.15 = (bf16[1,2,1,1,384,128]{5,4,3,2,1,0:T(8,128)(2,1)S(1)}, bf16[1,2,1,1,384,128]{5,4,3,2,1,0:T(8,128)(2,1)S(1)}, u32[]{:S(2)}, u32[]{:S(2)}) collective-permute-start(bf16[1,2,1,1,384,128]{5,4,3,2,1,0:T(8,128)(2,1)S(1)} %constant_dynamic-slice_fusion.8), channel_id=1, source_target_pairs={{0,16},{4,20},{8,24},{12,28},{16,0},{20,4},{24,8},{28,12},{1,17},{... | collective-permute-start | bytes 589832 | tf_op jit(solution)/shard_map/ppermute | solution.py:407
  362.3 18.3 %collective-permute-start.19 = (bf16[1,2,1,1,384,128]{5,4,3,2,1,0:T(8,128)(2,1)S(1)}, bf16[1,2,1,1,384,128]{5,4,3,2,1,0:T(8,128)(2,1)S(1)}, u32[]{:S(2)}, u32[]{:S(2)}) collective-permute-start(bf16[1,2,1,1,384,128]{5,4,3,2,1,0:T(8,128)(2,1)S(1)} %constant_dynamic-slice_fusion.4), channel_id=1, source_target_pairs={{0,16},{4,20},{8,24},{12,28},{16,0},{20,4},{24,8},{28,12},{1,17},{... | collective-permute-start | bytes 589832 | tf_op jit(solution)/shard_map/ppermute | solution.py:407
  375.5 12.3 %collective-permute-start.16 = (bf16[1,1,1,1,384,128]{5,4,3,2,1,0:T(8,128)(2,1)S(1)}, bf16[1,1,1,1,384,128]{5,4,3,2,1,0:T(8,128)(2,1)S(1)}, u32[]{:S(2)}, u32[]{:S(2)}) collective-permute-start(bf16[1,1,1,1,384,128]{5,4,3,2,1,0:T(8,128)(2,1)S(1)} %constant_dynamic-slice_fusion.7), channel_id=1, source_target_pairs={{0,8},{4,12},{8,0},{12,4},{16,24},{20,28},{24,16},{28,20},{1,9},{5... | collective-permute-start | bytes 294920 | tf_op jit(solution)/shard_map/ppermute | solution.py:407
  380.6 11.1 %collective-permute-start.20 = (bf16[1,1,1,1,384,128]{5,4,3,2,1,0:T(8,128)(2,1)S(1)}, bf16[1,1,1,1,384,128]{5,4,3,2,1,0:T(8,128)(2,1)S(1)}, u32[]{:S(2)}, u32[]{:S(2)}) collective-permute-start(bf16[1,1,1,1,384,128]{5,4,3,2,1,0:T(8,128)(2,1)S(1)} %constant_dynamic-slice_fusion.3), channel_id=1, source_target_pairs={{0,8},{4,12},{8,0},{12,4},{16,24},{20,28},{24,16},{28,20},{1,9},{5... | collective-permute-start | bytes 294920 | tf_op jit(solution)/shard_map/ppermute | solution.py:407
  433.2 5.7 %collective-permute-start.21 = (bf16[384,256]{1,0:T(8,128)(2,1)S(1)}, bf16[384,256]{1,0:T(8,128)(2,1)S(1)}, u32[]{:S(2)}, u32[]{:S(2)}) collective-permute-start(bf16[384,256]{1,0:T(8,128)(2,1)S(1)} %get-tuple-element.93), channel_id=1, source_target_pairs={{0,2},{2,0},{1,3},{3,1},{4,6},{6,4},{5,7},{7,5},{8,10},{10,8},{9,1... | collective-permute-start | bytes 589832 | tf_op jit(solution)/shard_map/ppermute | solution.py:441
  (9 other events, 14.9 us)
Sparse Core Ops, SparseCore 0:
  17.1 32.0 all-reduce.2
Sparse Core Ops, SparseCore 1:
  21.3 70.8 all-gather.2
  95.9 67.9 all-gather.4
  304.7 127.4 reduce-scatter.1

commit v3 on v2

--- a/solution.py
+++ b/solution.py
@@ -416,9 +416,10 @@
     return array
 
 
-def scatter_sum(blocks, dp, rows):
+def scatter_sum(blocks, dp, rows, earlier):
     array = from_blocks(blocks, dp, rows)
     array = exchange_half(array, 0, "tensor", 0)
+    array, earlier = lax.optimization_barrier((array, earlier))
     levels = dp.bit_length() - 1
     array = array.reshape((2,) * levels + (2, 6 * rows, COLS))
     last = levels - 1
@@ -434,7 +435,7 @@
         for level in range(levels - 1):
             one = exchange_half(one, level, "dp", levels - 1 - level)
         done.append(one.reshape(6 * rows, COLS // 2))
-    return jnp.concatenate(done, axis=1)
+    return jnp.concatenate(done, axis=1), earlier
 
 
 def swapped(array, axis):
@@ -524,7 +525,7 @@
         tiled=True,
     )
     back0 = run_backward(x_in, g_mid, smalls[0], hidden[0], mats[0], biases[0])
-    g0 = scatter_sum(back0[1], dp_n, rows)
+    g0, g1 = scatter_sum(back0[1], dp_n, rows, g1)
 
     other = swapped(jnp.where(first, g1, g0), "pipe")
     mine = jnp.where(first, g0, g1)

time: 458 us -> 489 us (1.068)
  waiting for transfers between devices: 197 us -> 227 us
    reduce_scatter x1, waiting for transfers between devices: 40.4 us -> 85.7 us  [on_device(): lax.psum_scatter(from_blocks(back1[1], dp_n, rows).reshape(-1, cols), ('t...]
    ppermute x9, waiting for transfers between devices: 51.5 us -> 35 us  [exchange_half(): there = lax.ppermute(half_of(array, 1 - which, axis), name, bits)]
  transfers between devices with their start and end apart: 26 -> 26, of which waited for: 17 -> 19; matrix products, arithmetic and copies ran while one was open for 10% -> 10% of each run, Pallas kernels for 5% -> 5%
where the time goes in v3:
time: 489 us; the launch traced here: 481 us
  waiting for transfers between devices  227 us (46%)
  Pallas kernels  149 us (30%)
  local copies, waits for them, and re-layouts  31.9 us (7%)
  starting transfers between devices  22.4 us (5%)
  between operations  18.3 us (4%)
  other arithmetic  16.4 us (3%)
  matrix products  16.2 us (3%)
    pallas_call x2, Pallas kernels, run_backward(): pl.pallas_call(bwd_kernel, out_shape=[shape(x.shape, BF16), shape((2, BLO...  125 us
    reduce_scatter x1, waiting for transfers between devices, on_device(): lax.psum_scatter(from_blocks(back1[1], dp_n, rows).reshape(-1, cols), ('t...  85.7 us
    all_gather x1, waiting for transfers between devices, on_device(): lax.all_gather(jnp.where(first, got, kept), ALL_AXES, axis=0, tiled=True)  44.7 us
    ppermute x9, waiting for transfers between devices, exchange_half(): there = lax.ppermute(half_of(array, 1 - which, axis), name, bits)  35 us
    unnamed x5, waiting for transfers between devices  25.1 us
    pallas_call x1, Pallas kernels, run_forward(): pl.pallas_call(fwd_kernel, out_shape=jax.ShapeDtypeStruct(x.shape, BF16),...  24.2 us
    all_gather x1, waiting for transfers between devices, on_device(): lax.all_gather(jnp.where(first, kept, got), ALL_AXES, axis=0, tiled=True)  24.2 us
  transfers between devices with their start and end apart: 26, of which 19 were waited for; matrix products, arithmetic and copies ran while one was open for 10% of the time, Pallas kernels for 5%

profile of v3, /device:TPU:0, one launch (start us, length us, event | category | flops | bytes accessed | tf_op | source)
XLA Modules:
  0.0 481.1 jit_solution(10735285554498450618)
XLA Ops:
  11.3 3.0 collective-permute-start.2
  17.0 2.2 collective-permute-done.2
  21.8 1.7 collective-permute-start
  24.6 24.6 %all-reduce.3.cloned.1.call-done = f32[23840]{0:T(1024)} async-done(((f32[23840]{0:T(1024)}), f32[23840]{0:T(1024)}) %all-reduce.3.cloned.1.call-update) | async-done | bytes 95376
  50.4 3.3 fusion.18
  54.2 3.3 fusion.24
  58.5 2.0 bitcast_select_fusion
  66.5 1.5 fusion.12.g_ref
  68.0 24.2 %all-gather.3.cloned.1.call-done = bf16[12288,256]{1,0:T(8,128)(2,1)} async-done(((bf16[384,256]{1,0:T(8,128)(2,1)}), bf16[12288,256]{1,0:T(8,128)(2,1)}) %all-gather.3.cloned.1.call-update) | async-done | bytes 6291472 | tf_op jit(solution)/shard_map/all_gather | solution.py:462
  92.2 2.8 copy-done.3
  95.0 24.2 %shard_map.302 = bf16[4,256,512]{2,1,0:T(8,128)(2,1)S(1)} custom-call(bf16[4,256,512]{2,1,0:T(8,128)(2,1)S(1)} %fusion.11.x_ref, f32[8,512]{1,0:T(8,128)S(1)} %concatenate.83.small_ref, f32[1,2048]{1,0:T(1,128)S(1)} %bitcast.170, bf16[8,2,768,256]{3,2,1,0:T(8,128)(2,1)S(1)} %bitcast.173, f32[1,4,64,256]{3,2,1,0:T(8,128)S(1)} %reshape.347.bias_ref), custom_call_target="tpu_custom_call" | custom-call | flops 19327352832 | bytes 20000000 | tf_op jit(solution)/shard_map/pallas_call | solution.py:320
  119.2 44.7 %all-gather.5.cloned.1.call-done = bf16[12288,256]{1,0:T(8,128)(2,1)} async-done(((bf16[384,256]{1,0:T(8,128)(2,1)}), bf16[12288,256]{1,0:T(8,128)(2,1)}) %all-gather.5.cloned.1.call-update) | async-done | bytes 6291472 | tf_op jit(solution)/shard_map/all_gather | solution.py:463
  163.9 1.4 fusion.13.x_ref
  165.3 62.5 %shard_map.303 = (bf16[4,256,512]{2,1,0:T(8,128)(2,1)}, bf16[2,8,768,256]{3,2,1,0:T(8,128)(2,1)}, f32[8,512]{1,0:T(8,128)}, f32[1,2048]{1,0:T(1,128)}, f32[4,64,256]{2,1,0:T(8,128)}) custom-call(bf16[4,256,512]{2,1,0:T(8,128)(2,1)} %fusion.13.x_ref, bf16[4,256,512]{2,1,0:T(8,128)(2,1)} %fusion.12.g_ref, f32[8,512]{1,0:T(8,128)} %concatenate.86.small_ref, ...), custom_call_target="tpu_custom_call" | custom-call | flops 57982058496 | bytes 20000000 | tf_op jit(solution)/shard_map/pallas_call | solution.py:342
  227.9 2.6 fusion.14.g_ref
  230.5 62.0 %shard_map.304 = (bf16[4,256,512]{2,1,0:T(8,128)(2,1)}, bf16[2,8,768,256]{3,2,1,0:T(8,128)(2,1)}, f32[8,512]{1,0:T(8,128)}, f32[1,2048]{1,0:T(1,128)}, f32[4,64,256]{2,1,0:T(8,128)}) custom-call(bf16[4,256,512]{2,1,0:T(8,128)(2,1)} %copy-done.4, bf16[4,256,512]{2,1,0:T(8,128)(2,1)} %fusion.14.g_ref, f32[8,512]{1,0:T(8,128)} %copy-done.1, ...), custom_call_target="tpu_custom_call" | custom-call | flops 57982058496 | bytes 20000000 | tf_op jit(solution)/shard_map/pallas_call | solution.py:342
  294.0 1.4 fusion.6
  296.1 1.4 fusion.5
  299.2 1.5 collective-permute-start.8
  300.7 2.3 constant_dynamic-slice_fusion.11
  303.8 1.5 collective-permute-start.9
  305.7 2.5 collective-permute-done.9
  308.2 1.6 collective-permute-start.10
  310.9 1.7 collective-permute-done.10
  312.6 1.9 collective-permute-start.11
  315.4 2.5 collective-permute-done.11
  319.4 3.8 add_convert_fusion
  323.2 85.7 %reduce-scatter.2.cloned.1.call-done = bf16[384,256]{1,0:T(8,128)(2,1)} async-done(((bf16[12288,256]{1,0:T(8,128)(2,1)}), bf16[384,256]{1,0:T(8,128)(2,1)}) %reduce-scatter.2.cloned.1.call-update) | async-done | bytes 196624 | tf_op jit(solution)/shard_map/reduce_scatter | solution.py:521
  409.0 1.7 fusion.43
  410.6 1.2 copy-done.6
  412.8 1.3 collective-permute-start.13
  415.4 1.4 collective-permute-start.17
  416.8 1.2 bitcast_select_fusion.5
  418.0 1.2 bitcast_select_fusion.3
  419.2 11.4 %collective-permute-done.13 = bf16[2,2,2,1,384,128]{5,4,3,2,1,0:T(8,128)(2,1)} collective-permute-done((bf16[2,2,2,1,384,128]{5,4,3,2,1,0:T(8,128)(2,1)}, bf16[2,2,2,1,384,128]{5,4,3,2,1,0:T(8,128)(2,1)}, u32[]{:S(2)}, u32[]{:S(2)}) %collective-permute-start.13) | collective-permute-done | bytes 786464 | tf_op jit(solution)/shard_map/ppermute | solution.py:407
  430.6 1.3 add_convert_fusion.2
  432.0 1.5 collective-permute-start.14
  434.0 1.3 collective-permute-start.18
  436.6 4.7 collective-permute-done.14
  441.4 1.7 collective-permute-start.15
  443.1 3.1 collective-permute-done.18
  446.3 1.6 collective-permute-start.19
  447.9 8.0 %collective-permute-done.15 = bf16[1,2,1,1,384,128]{5,4,3,2,1,0:T(8,128)(2,1)S(1)} collective-permute-done((bf16[1,2,1,1,384,128]{5,4,3,2,1,0:T(8,128)(2,1)S(1)}, bf16[1,2,1,1,384,128]{5,4,3,2,1,0:T(8,128)(2,1)S(1)}, u32[]{:S(2)}, u32[]{:S(2)}) %collective-permute-start.15) | collective-permute-done | bytes 196640 | tf_op jit(solution)/shard_map/ppermute | solution.py:407
  456.0 3.1 collective-permute-done.19
  459.3 2.0 collective-permute-done.16
  461.4 2.5 collective-permute-done.20
  465.8 1.7 copy.85
  467.5 2.3 collective-permute-done.21
  (218 shorter events, 34.8 us)
Async XLA Ops:
  8.0 6.5 %copy-start.36 = (u32[32]{0:T(128)S(1)}, u32[32]{0:T(128)}, u32[]{:S(2)}) copy-start(u32[32]{0:T(128)} %constant.91) | copy-start | bytes 388
  8.0 6.3 %copy-start.28 = (f32[1,2,512]{2,1,0:T(2,128)S(1)}, f32[1,2,512]{2,1,0:T(2,128)}, u32[]{:S(2)}) copy-start(f32[1,2,512]{2,1,0:T(2,128)} %param.25) | copy-start | bytes 12292
  8.0 6.3 %copy-start.29 = (f32[1,2,512]{2,1,0:T(2,128)S(1)}, f32[1,2,512]{2,1,0:T(2,128)}, u32[]{:S(2)}) copy-start(f32[1,2,512]{2,1,0:T(2,128)} %param.26) | copy-start | bytes 12292
  8.0 6.3 %copy-start.30 = (f32[1,2,512]{2,1,0:T(2,128)S(1)}, f32[1,2,512]{2,1,0:T(2,128)}, u32[]{:S(2)}) copy-start(f32[1,2,512]{2,1,0:T(2,128)} %param.31) | copy-start | bytes 12292
  8.1 6.3 %copy-start.32 = (f32[1,2,256]{2,1,0:T(2,128)S(1)}, f32[1,2,256]{2,1,0:T(2,128)}, u32[]{:S(2)}) copy-start(f32[1,2,256]{2,1,0:T(2,128)} %param.28) | copy-start | bytes 6148
  8.1 6.3 %copy-start.27 = (f32[1,8,169]{2,1,0:T(8,128)S(1)}, f32[1,8,169]{2,1,0:T(8,128)}, u32[]{:S(2)}) copy-start(f32[1,8,169]{2,1,0:T(8,128)} %param.29) | copy-start | bytes 16228
  8.1 7.7 %copy-start.31 = (f32[1,1024]{1,0:T(1,128)S(1)}, f32[1,1024]{1,0:T(1,128)}, u32[]{:S(2)}) copy-start(f32[1,1024]{1,0:T(1,128)} %param.33) | copy-start | bytes 12292
  8.1 41.1 %all-reduce.3.cloned.1.call-start = ((), (), s32[]{:S(2)}) async-start(), calls=%async_computation.4 | async-start | bytes 196608
  9.1 11.5 %copy-start.13 = (bf16[1,98,16,512]{3,2,1,0:T(8,128)(2,1)S(1)}, bf16[1,98,16,512]{3,2,1,0:T(8,128)(2,1)}, u32[]{:S(2)}) copy-start(bf16[1,98,16,512]{3,2,1,0:T(8,128)(2,1)} %param.23) | copy-start | bytes 4816900
  11.3 7.9 %collective-permute-start.2 = (bf16[384,256]{1,0:T(8,128)(2,1)S(1)}, bf16[384,256]{1,0:T(8,128)(2,1)S(1)}, u32[]{:S(2)}, u32[]{:S(2)}) collective-permute-start(bf16[384,256]{1,0:T(8,128)(2,1)S(1)} %constant_dynamic-slice_fusion.13), channel_id=1, source_target_pairs={{0,2},{2,0},{1,3},{3,1},{4,6},{6,4},{5,7},{7,5},{8,10},{10,8},{9,1... | collective-permute-start | bytes 589832 | tf_op jit(solution)/shard_map/ppermute | solution.py:442
  17.0 75.2 %all-gather.3.cloned.1.call-start = ((), (), s32[]{:S(2)}) async-start(), calls=%async_computation.1 | async-start | bytes 6488064 | tf_op jit(solution)/shard_map/all_gather | solution.py:462
  20.0 143.9 %all-gather.5.cloned.1.call-start = ((), (), s32[]{:S(2)}) async-start(), calls=%async_computation.2 | async-start | bytes 6488064 | tf_op jit(solution)/shard_map/all_gather | solution.py:463
  20.6 388.3 %reduce-scatter.2.cloned.1.call-start = ((), (), s32[]{:S(2)}) async-start(), calls=%async_computation.3 | async-start | bytes 6488064 | tf_op jit(solution)/shard_map/reduce_scatter | solution.py:521
  21.8 28.6 %copy-start.34 = (s32[64,64]{1,0:T(8,128)S(1)}, s32[64,64]{1,0:T(8,128)}, u32[]{:S(2)}) copy-start(s32[64,64]{1,0:T(8,128)} %constant.69.clone) | copy-start | bytes 49156
  21.8 36.7 %collective-permute-start = (bf16[98,8,512]{2,1,0:T(8,128)(2,1)}, bf16[98,8,512]{2,1,0:T(8,128)(2,1)}, u32[]{:S(2)}, u32[]{:S(2)}) collective-permute-start(bf16[98,8,512]{2,1,0:T(8,128)(2,1)} %get-tuple-element.83), channel_id=1, source_target_pairs={{0,2},{2,0},{1,3},{3,1},{4,6},{6,4},{5,7},{7,5},{8,10},{10,8},{9,1... | collective-permute-start | bytes 2408456 | tf_op jit(solution)/shard_map/ppermute | solution.py:442
  54.1 38.1 %copy-start = (f32[1,4,64,256]{3,2,1,0:T(8,128)}, f32[1,4,64,256]{3,2,1,0:T(8,128)S(1)}, u32[]{:S(2)}) copy-start(f32[1,4,64,256]{3,2,1,0:T(8,128)S(1)} %reshape.347.bias_ref) | copy-start | bytes 786436
  54.1 38.1 %copy-start.2 = (f32[1,1,2,1024]{3,1,2,0:T(1,128)}, f32[1,1,2,1024]{3,1,2,0:T(1,128)S(1)}, u32[]{:S(2)}) copy-start(f32[1,1,2,1024]{3,1,2,0:T(1,128)S(1)} %copy.100) | copy-start | bytes 24580
  61.3 3.1 collective-permute-start.1
  62.1 2.3 collective-permute-start.3
  62.7 29.5 %copy-start.1 = (f32[8,512]{1,0:T(8,128)}, f32[8,512]{1,0:T(8,128)S(1)}, u32[]{:S(2)}) copy-start(f32[8,512]{1,0:T(8,128)S(1)} %concatenate.83.small_ref) | copy-start | bytes 49156
  66.1 53.1 %copy-start.4 = (bf16[4,256,512]{2,1,0:T(8,128)(2,1)}, bf16[4,256,512]{2,1,0:T(8,128)(2,1)S(1)}, u32[]{:S(2)}) copy-start(bf16[4,256,512]{2,1,0:T(8,128)(2,1)S(1)} %fusion.11.x_ref) | copy-start | bytes 3145732
  94.9 69.0 %copy-start.21 = (bf16[256,256,1]{1,0,2:T(8,128)(2,1)S(1)}, bf16[256,256,1]{1,0,2:T(8,128)(2,1)}, u32[]{:S(2)}) copy-start(bf16[256,256,1]{1,0,2:T(8,128)(2,1)} %constant.96) | copy-start | bytes 393220
  165.3 62.5 %copy-start.20 = (bf16[256,256,1]{1,0,2:T(8,128)(2,1)S(1)}, bf16[256,256,1]{1,0,2:T(8,128)(2,1)}, u32[]{:S(2)}) copy-start(bf16[256,256,1]{1,0,2:T(8,128)(2,1)} %constant.98) | copy-start | bytes 393220
  297.8 1.3 collective-permute-start.7
  298.5 16.0 %copy-start.9 = (bf16[4,512,196]{1,2,0:T(8,128)(2,1)}, bf16[4,512,196]{1,2,0:T(8,128)(2,1)S(1)}, u32[]{:S(2)}) copy-start(bf16[4,512,196]{1,2,0:T(8,128)(2,1)S(1)} %convolution_convert_fusion.4) | copy-start | bytes 2408452
  299.2 4.5 collective-permute-start.8
  303.0 16.4 %collective-permute-start.12 = (bf16[1,8,768,256]{3,2,1,0:T(8,128)(2,1)S(1)}, bf16[1,8,768,256]{3,2,1,0:T(8,128)(2,1)}, u32[]{:S(2)}, u32[]{:S(2)}) collective-permute-start(bf16[1,8,768,256]{3,2,1,0:T(8,128)(2,1)S(1)} %constant_dynamic-slice_fusion.11), channel_id=1, source_target_pairs={{0,1},{1,0},{2,3},{3,2},{4,5},{5,4},{6,7},{7,6},{8,9},{9,8},{10,11... | collective-permute-start | bytes 9437192 | tf_op jit(solution)/shard_map/ppermute | solution.py:407
  303.8 4.4 collective-permute-start.9
  305.6 9.7 %copy-start.11 = (bf16[4,512,196]{1,2,0:T(8,128)(2,1)}, bf16[4,512,196]{1,2,0:T(8,128)(2,1)S(1)}, u32[]{:S(2)}) copy-start(bf16[4,512,196]{1,2,0:T(8,128)(2,1)S(1)} %convolution_convert_fusion.5) | copy-start | bytes 2408452
  308.2 4.4 collective-permute-start.10
  310.6 106.1 %collective-permute-start.4 = (bf16[98,4,512]{2,0,1:T(8,128)(2,1)}, bf16[98,4,512]{2,0,1:T(8,128)(2,1)}, u32[]{:S(2)}, u32[]{:S(2)}) collective-permute-start(bf16[98,4,512]{2,0,1:T(8,128)(2,1)} %dynamic-slice_bitcast_fusion.2), channel_id=1, source_target_pairs={{0,1},{1,0},{2,3},{3,2},{4,5},{5,4},{6,7},{7,6},{8,9},{9,8},{10,11... | collective-permute-start | bytes 1204232 | tf_op jit(solution)/shard_map/ppermute | solution.py:442
  312.6 5.3 %collective-permute-start.11 = (f32[2,8848]{1,0:T(2,128)S(1)}, f32[2,8848]{1,0:T(2,128)S(1)}, u32[]{:S(2)}, u32[]{:S(2)}) collective-permute-start(f32[2,8848]{1,0:T(2,128)S(1)} %add.221), channel_id=1, source_target_pairs={{0,16},{4,20},{8,24},{12,28},{16,0},{20,4},{24,8},{28,12},{1,17},{... | collective-permute-start | bytes 212360 | tf_op jit(solution)/shard_map/ppermute | solution.py:415
  315.4 102.6 %collective-permute-start.5 = (bf16[98,4,512]{2,0,1:T(8,128)(2,1)}, bf16[98,4,512]{2,0,1:T(8,128)(2,1)}, u32[]{:S(2)}, u32[]{:S(2)}) collective-permute-start(bf16[98,4,512]{2,0,1:T(8,128)(2,1)} %dynamic-slice_bitcast_fusion.1), channel_id=1, source_target_pairs={{0,1},{1,0},{2,3},{3,2},{4,5},{5,4},{6,7},{7,6},{8,9},{9,8},{10,11... | collective-permute-start | bytes 1204232 | tf_op jit(solution)/shard_map/ppermute | solution.py:442
  410.6 4.7 copy-start.5
  410.6 6.1 %copy-start.12 = (bf16[4,512,196]{1,2,0:T(8,128)(2,1)S(1)}, bf16[4,512,196]{1,2,0:T(8,128)(2,1)}, u32[]{:S(2)}) copy-start(bf16[4,512,196]{1,2,0:T(8,128)(2,1)} %copy-done.11) | copy-start | bytes 2408452
  412.8 5.2 %copy-start.10 = (bf16[4,512,196]{1,2,0:T(8,128)(2,1)S(1)}, bf16[4,512,196]{1,2,0:T(8,128)(2,1)}, u32[]{:S(2)}) copy-start(bf16[4,512,196]{1,2,0:T(8,128)(2,1)} %copy-done.9) | copy-start | bytes 2408452
  412.8 17.8 %collective-permute-start.13 = (bf16[2,2,2,1,384,128]{5,4,3,2,1,0:T(8,128)(2,1)}, bf16[2,2,2,1,384,128]{5,4,3,2,1,0:T(8,128)(2,1)}, u32[]{:S(2)}, u32[]{:S(2)}) collective-permute-start(bf16[2,2,2,1,384,128]{5,4,3,2,1,0:T(8,128)(2,1)} %constant_dynamic-slice_fusion.10), channel_id=1, source_target_pairs={{0,2},{2,0},{1,3},{3,1},{4,6},{6,4},{5,7},{7,5},{8,10},{10,8},{9,1... | collective-permute-start | bytes 2359304 | tf_op jit(solution)/shard_map/ppermute | solution.py:407
  415.4 15.2 %copy-start.7 = (bf16[2,2,2,2,384,128]{5,4,3,2,1,0:T(8,128)(2,1)S(1)}, bf16[2,2,2,2,384,128]{5,4,3,2,1,0:T(8,128)(2,1)}, u32[]{:S(2)}) copy-start(bf16[2,2,2,2,384,128]{5,4,3,2,1,0:T(8,128)(2,1)} %copy-done.6) | copy-start | bytes 4718596
  415.4 18.4 %collective-permute-start.17 = (bf16[2,2,1,2,384,128]{5,4,3,2,1,0:T(8,128)(2,1)S(1)}, bf16[2,2,1,2,384,128]{5,4,3,2,1,0:T(8,128)(2,1)S(1)}, u32[]{:S(2)}, u32[]{:S(2)}) collective-permute-start(bf16[2,2,1,2,384,128]{5,4,3,2,1,0:T(8,128)(2,1)S(1)} %constant_dynamic-slice_fusion.6), channel_id=1, source_target_pairs={{0,4},{4,0},{8,12},{12,8},{16,20},{20,16},{24,28},{28,24},{1,5},{5... | collective-permute-start | bytes 2359304 | tf_op jit(solution)/shard_map/ppermute | solution.py:407
  432.0 9.2 %collective-permute-start.14 = (bf16[2,2,1,1,384,128]{5,4,3,2,1,0:T(8,128)(2,1)S(1)}, bf16[2,2,1,1,384,128]{5,4,3,2,1,0:T(8,128)(2,1)S(1)}, u32[]{:S(2)}, u32[]{:S(2)}) collective-permute-start(bf16[2,2,1,1,384,128]{5,4,3,2,1,0:T(8,128)(2,1)S(1)} %constant_dynamic-slice_fusion.9), channel_id=1, source_target_pairs={{0,4},{4,0},{8,12},{12,8},{16,20},{20,16},{24,28},{28,24},{1,5},{5... | collective-permute-start | bytes 1179656 | tf_op jit(solution)/shard_map/ppermute | solution.py:407
  434.0 12.1 %collective-permute-start.18 = (bf16[2,2,1,1,384,128]{5,4,3,2,1,0:T(8,128)(2,1)S(1)}, bf16[2,2,1,1,384,128]{5,4,3,2,1,0:T(8,128)(2,1)S(1)}, u32[]{:S(2)}, u32[]{:S(2)}) collective-permute-start(bf16[2,2,1,1,384,128]{5,4,3,2,1,0:T(8,128)(2,1)S(1)} %constant_dynamic-slice_fusion.5), channel_id=1, source_target_pairs={{0,2},{2,0},{1,3},{3,1},{4,6},{6,4},{5,7},{7,5},{8,10},{10,8},{9,1... | collective-permute-start | bytes 1179656 | tf_op jit(solution)/shard_map/ppermute | solution.py:407
  435.7 29.6 %collective-permute-start.6 = (bf16[98,8,512]{2,1,0:T(8,128)(2,1)S(1)}, bf16[98,8,512]{2,1,0:T(8,128)(2,1)S(1)}, u32[]{:S(2)}, u32[]{:S(2)}) collective-permute-start(bf16[98,8,512]{2,1,0:T(8,128)(2,1)S(1)} %copy.79), channel_id=1, source_target_pairs={{0,2},{2,0},{1,3},{3,1},{4,6},{6,4},{5,7},{7,5},{8,10},{10,8},{9,1... | collective-permute-start | bytes 2408456 | tf_op jit(solution)/shard_map/ppermute | solution.py:442
  441.4 22.6 %copy-start.19 = (bf16[384,256]{1,0:T(8,128)(2,1)S(1)}, bf16[384,256]{1,0:T(8,128)(2,1)}, u32[]{:S(2)}) copy-start(bf16[384,256]{1,0:T(8,128)(2,1)} %reduce-scatter.2.cloned.1.call-done) | copy-start | bytes 589828
  441.4 14.5 %collective-permute-start.15 = (bf16[1,2,1,1,384,128]{5,4,3,2,1,0:T(8,128)(2,1)S(1)}, bf16[1,2,1,1,384,128]{5,4,3,2,1,0:T(8,128)(2,1)S(1)}, u32[]{:S(2)}, u32[]{:S(2)}) collective-permute-start(bf16[1,2,1,1,384,128]{5,4,3,2,1,0:T(8,128)(2,1)S(1)} %constant_dynamic-slice_fusion.8), channel_id=1, source_target_pairs={{0,16},{4,20},{8,24},{12,28},{16,0},{20,4},{24,8},{28,12},{1,17},{... | collective-permute-start | bytes 589832 | tf_op jit(solution)/shard_map/ppermute | solution.py:407
  446.3 12.9 %collective-permute-start.19 = (bf16[1,2,1,1,384,128]{5,4,3,2,1,0:T(8,128)(2,1)S(1)}, bf16[1,2,1,1,384,128]{5,4,3,2,1,0:T(8,128)(2,1)S(1)}, u32[]{:S(2)}, u32[]{:S(2)}) collective-permute-start(bf16[1,2,1,1,384,128]{5,4,3,2,1,0:T(8,128)(2,1)S(1)} %constant_dynamic-slice_fusion.4), channel_id=1, source_target_pairs={{0,16},{4,20},{8,24},{12,28},{16,0},{20,4},{24,8},{28,12},{1,17},{... | collective-permute-start | bytes 589832 | tf_op jit(solution)/shard_map/ppermute | solution.py:407
  456.0 5.4 %collective-permute-start.16 = (bf16[1,1,1,1,384,128]{5,4,3,2,1,0:T(8,128)(2,1)S(1)}, bf16[1,1,1,1,384,128]{5,4,3,2,1,0:T(8,128)(2,1)S(1)}, u32[]{:S(2)}, u32[]{:S(2)}) collective-permute-start(bf16[1,1,1,1,384,128]{5,4,3,2,1,0:T(8,128)(2,1)S(1)} %constant_dynamic-slice_fusion.7), channel_id=1, source_target_pairs={{0,8},{4,12},{8,0},{12,4},{16,24},{20,28},{24,16},{28,20},{1,9},{5... | collective-permute-start | bytes 294920 | tf_op jit(solution)/shard_map/ppermute | solution.py:407
  459.2 4.7 collective-permute-start.20
  464.0 5.7 %collective-permute-start.21 = (bf16[384,256]{1,0:T(8,128)(2,1)S(1)}, bf16[384,256]{1,0:T(8,128)(2,1)S(1)}, u32[]{:S(2)}, u32[]{:S(2)}) collective-permute-start(bf16[384,256]{1,0:T(8,128)(2,1)S(1)} %get-tuple-element.97), channel_id=1, source_target_pairs={{0,2},{2,0},{1,3},{3,1},{4,6},{6,4},{5,7},{7,5},{8,10},{10,8},{9,1... | collective-permute-start | bytes 589832 | tf_op jit(solution)/shard_map/ppermute | solution.py:442
  (15 other events, 29.9 us)
Sparse Core Ops, SparseCore 0:
  17.1 32.0 all-reduce.2
Sparse Core Ops, SparseCore 1:
  21.3 70.8 all-gather.2
  95.9 67.9 all-gather.4
  292.6 116.3 reduce-scatter.1
